TPU v7x, 128 devices: a whole 4x4x4 slice. The times are simulated.
128 devices in a mesh: gauss: 8 (over y, core), render: 16 (over x, z).
Axes of the slice: x: 4, y: 4, z: 4, core: 2. Of those that a mesh axis runs over, the one named last changes fastest.
Arguments:
- params: float32 [59, 262144], P(None, ('gauss', 'render')), as said below
- first_moment: float32 [59, 262144], P(None, ('gauss', 'render')), may hold values from -1.5 to 1.5
- second_moment: float32 [59, 262144], P(None, ('gauss', 'render')), may hold values from 0.0001 to 0.01
- target_images: float32 [4096, 3, 256], P(('gauss', 'render')), may hold values from 0 to 1
- tile_lists: int32 [4096, 512], P(('gauss', 'render')), may hold values from -1 to 16383, as said below
- send_index: int32 [128, 128, 128], P(('gauss', 'render')), may hold values from 0 to 2047, as said below
Outputs:
- images: float32 [4096, 3, 256], P(('gauss', 'render'))
- new_params: float32 [59, 262144], P(None, ('gauss', 'render'))
- new_first: float32 [59, 262144], P(None, ('gauss', 'render'))
- new_second: float32 [59, 262144], P(None, ('gauss', 'render'))
Inputs may be any that keep to these rules, and one draw needn't show every extreme that they name: `tile_lists`: A live entry names slot s * 128 + j of its device's received slots: the j-th Gaussian that device s sends it. Each tile's live entries come first, at least 64 of them; every tile of some device has all 512 entries live. On one device every named slot is named by exactly one entry. send_index[s, d, j] is the local index on owner s of the Gaussian sent as slot j to renderer d; slots that no list of d names hold 0. No Gaussian is sent twice to one renderer. Some renderer uses every slot from every owner. `params`: row 6, the quaternion's real part, lies between 1 and 2.
All inputs are finite; a program needn't handle non-finite values.
Results may differ from a plain program's by a relative error of at most 0.0003.
Values sent between devices are 32-bit elements; how exact they have to be, the bound alone decides.
A program may use at most 128 MiB of HBM per device.

v0:
```python
import math

import jax
import jax.numpy as jnp
import numpy as np
from jax import lax
from jax.sharding import PartitionSpec as P

PARAMS = 59
PIX = 256
VIEWS = 16
TILE_COLS = 8
GROUP = 4


sh_first = 0.28209479177387814
sh_second = 0.4886025119029199
sh_third = (
    1.0925484305920792,
    -1.0925484305920792,
    0.31539156525252005,
    -1.0925484305920792,
    0.5462742152960396,
)
sh_fourth = (
    -0.5900435899266435,
    2.890611442640554,
    -0.4570457994644658,
    0.3731763325901154,
    -0.4570457994644658,
    1.445305721320277,
    -0.5900435899266435,
)
tilt_reach = 0.25
beta_one = 0.9
beta_two = 0.999
adam_epsilon = 1e-15
adam_count = 1000.0


def learning_rates():
    table = np.full((PARAMS,), 0.000125)
    table[0:3] = 0.0016
    table[3:6] = 0.005
    table[6:10] = 0.001
    table[10] = 0.05
    table[11] = 0.0025
    table[27] = 0.0025
    table[43] = 0.0025
    return jnp.asarray(table, dtype=jnp.float32)


def sh_basis(dir_x, dir_y, dir_z):
    sq_x = dir_x * dir_x
    sq_y = dir_y * dir_y
    sq_z = dir_z * dir_z
    return [
        sh_first * jnp.ones_like(dir_x),
        -sh_second * dir_y,
        sh_second * dir_z,
        -sh_second * dir_x,
        sh_third[0] * dir_x * dir_y,
        sh_third[1] * dir_y * dir_z,
        sh_third[2] * (2.0 * sq_z - sq_x - sq_y),
        sh_third[3] * dir_x * dir_z,
        sh_third[4] * (sq_x - sq_y),
        sh_fourth[0] * dir_y * (3.0 * sq_x - sq_y),
        sh_fourth[1] * dir_x * dir_y * dir_z,
        sh_fourth[2] * dir_y * (4.0 * sq_z - sq_x - sq_y),
        sh_fourth[3] * dir_z * (2.0 * sq_z - 3.0 * sq_x - 3.0 * sq_y),
        sh_fourth[4] * dir_x * (4.0 * sq_z - sq_x - sq_y),
        sh_fourth[5] * dir_z * (sq_x - sq_y),
        sh_fourth[6] * dir_x * (sq_x - 3.0 * sq_y),
    ]


def project(raw_params, camera):
    angle = camera.astype(jnp.float32) * (2.0 * math.pi / VIEWS)
    lean_x = tilt_reach * jnp.cos(angle)
    lean_y = tilt_reach * jnp.sin(angle)
    shift_x = 16.0 * (camera % 4).astype(jnp.float32)
    shift_y = 16.0 * (camera // 4).astype(jnp.float32)
    length = jnp.sqrt(1.0 + lean_x * lean_x + lean_y * lean_y)
    basis = sh_basis(lean_x / length, lean_y / length, -1.0 / length)
    screen_x = raw_params[0] + lean_x * raw_params[2] - shift_x
    screen_y = raw_params[1] + lean_y * raw_params[2] - shift_y
    squares = [jnp.exp(2.0 * raw_params[3 + axis_position]) for axis_position in range(3)]
    quat_norm = jnp.sqrt(
        raw_params[6] * raw_params[6]
        + raw_params[7] * raw_params[7]
        + raw_params[8] * raw_params[8]
        + raw_params[9] * raw_params[9]
    )
    q_w = raw_params[6] / quat_norm
    q_x = raw_params[7] / quat_norm
    q_y = raw_params[8] / quat_norm
    q_z = raw_params[9] / quat_norm
    rotation = [
        [
            1.0 - 2.0 * (q_y * q_y + q_z * q_z),
            2.0 * (q_x * q_y - q_w * q_z),
            2.0 * (q_x * q_z + q_w * q_y),
        ],
        [
            2.0 * (q_x * q_y + q_w * q_z),
            1.0 - 2.0 * (q_x * q_x + q_z * q_z),
            2.0 * (q_y * q_z - q_w * q_x),
        ],
        [
            2.0 * (q_x * q_z - q_w * q_y),
            2.0 * (q_y * q_z + q_w * q_x),
            1.0 - 2.0 * (q_x * q_x + q_y * q_y),
        ],
    ]
    footprint_spread = [
        [
            rotation[row_at][0] * rotation[col_at][0] * squares[0]
            + rotation[row_at][1] * rotation[col_at][1] * squares[1]
            + rotation[row_at][2] * rotation[col_at][2] * squares[2]
            for col_at in range(3)
        ]
        for row_at in range(3)
    ]
    cov_xx = (
        footprint_spread[0][0]
        + 2.0 * lean_x * footprint_spread[0][2]
        + lean_x * lean_x * footprint_spread[2][2]
        + 0.3
    )
    cov_xy = (
        footprint_spread[0][1]
        + lean_x * footprint_spread[1][2]
        + lean_y * footprint_spread[0][2]
        + lean_x * lean_y * footprint_spread[2][2]
    )
    cov_yy = (
        footprint_spread[1][1]
        + 2.0 * lean_y * footprint_spread[1][2]
        + lean_y * lean_y * footprint_spread[2][2]
        + 0.3
    )
    determinant = cov_xx * cov_yy - cov_xy * cov_xy
    opacity = jax.nn.sigmoid(raw_params[10])
    colours = [
        jnp.maximum(
            0.5 + sum((raw_params[11 + 16 * channel + term] * basis[term] for term in range(16))),
            0.0,
        )
        for channel in range(3)
    ]
    screen_x, screen_y, opacity = jnp.broadcast_arrays(screen_x, screen_y, opacity)
    stacked = [
        screen_x,
        screen_y,
        cov_yy / determinant,
        -cov_xy / determinant,
        cov_xx / determinant,
        opacity,
    ] + colours
    return jnp.stack(jnp.broadcast_arrays(*stacked))


def tile_corner_points(placed):
    anchor_x = 16.0 * (placed % TILE_COLS).astype(jnp.float32)
    anchor_y = 16.0 * (placed // TILE_COLS).astype(jnp.float32)
    return (anchor_x, anchor_y)


def composite(feature_vectors, live_mask, anchor_x, anchor_y):
    pixels = jnp.arange(PIX, dtype=jnp.int32)
    offset_x = (pixels % 16).astype(jnp.float32) + 0.5
    offset_y = (pixels // 16).astype(jnp.float32) + 0.5
    delta_x = anchor_x[:, None, None] + offset_x[None, None, :] - feature_vectors[:, 0, :, None]
    delta_y = anchor_y[:, None, None] + offset_y[None, None, :] - feature_vectors[:, 1, :, None]
    exponent = (
        -0.5
        * (
            feature_vectors[:, 2, :, None] * delta_x * delta_x
            + feature_vectors[:, 4, :, None] * delta_y * delta_y
        )
        - feature_vectors[:, 3, :, None] * delta_x * delta_y
    )
    alpha_values = (
        jnp.minimum(feature_vectors[:, 5, :, None] * jnp.exp(exponent), 0.99)
        * live_mask[:, :, None]
    )
    log_keep = jnp.log(1.0 - alpha_values)
    transmittance = jnp.exp(jnp.cumsum(log_keep, axis=1) - log_keep)
    return jnp.einsum(
        "dwo,doy->dwy",
        feature_vectors[:, 6:9, :],
        alpha_values * transmittance,
        precision=lax.Precision.HIGHEST,
    )


def render_tiles(feature_vectors, live_mask, anchor_x, anchor_y, target):
    groups = feature_vectors.shape[0] // GROUP

    def one_group(bundle):
        feats_g, live_g, tile_left_edge, top_edge, target_g = bundle
        shaded, pullback = jax.vjp(
            lambda values: composite(values, live_g, tile_left_edge, top_edge), feats_g
        )
        (feat_grad,) = pullback(shaded - target_g)
        return (shaded, feat_grad)

    bundle = tuple(
        (
            member.reshape((groups, GROUP) + member.shape[1:])
            for member in (feature_vectors, live_mask, anchor_x, anchor_y, target)
        )
    )
    shaded, feat_grad = lax.map(one_group, bundle)
    return (shaded.reshape(target.shape), feat_grad.reshape(feature_vectors.shape))


def adam_step(params, first_moment, second_moment, gradient):
    rates = learning_rates()
    new_first = beta_one * first_moment + (1.0 - beta_one) * gradient
    new_second = beta_two * second_moment + (1.0 - beta_two) * gradient * gradient
    first_hat = new_first / (1.0 - beta_one**adam_count)
    second_hat = new_second / (1.0 - beta_two**adam_count)
    new_params = params - rates[:, None] * first_hat / (jnp.sqrt(second_hat) + adam_epsilon)
    return (new_params, new_first, new_second)


def deliver(outgoing):
    arrived = lax.all_to_all(outgoing, ("gauss", "render"), split_axis=1, concat_axis=1, tiled=True)
    return arrived


def give_back(returning):
    arrived = lax.all_to_all(
        returning, ("gauss", "render"), split_axis=1, concat_axis=1, tiled=True
    )
    return arrived


def per_device(params, first_moment, second_moment, target_images, tile_lists, send_index):
    devices = lax.axis_size("gauss") * lax.axis_size("render")
    device = lax.axis_index(("gauss", "render"))
    per_view = devices // VIEWS
    tiles_here = tile_lists.shape[0]
    chosen = send_index[0]
    outgoing = params[:, chosen]
    own_camera = device // per_view
    received = deliver(outgoing)
    buffer, render_pull = jax.vjp(lambda values: project(values, own_camera), received)
    columns = buffer.shape[2]
    slot_table = buffer.reshape(9, devices * columns)
    entry_idx = jnp.maximum(tile_lists, 0)
    live_mask = (tile_lists >= 0).astype(jnp.float32)
    placed = device % per_view * tiles_here + jnp.arange(tiles_here, dtype=jnp.int32)
    anchor_x, anchor_y = tile_corner_points(placed)
    shaded, feat_grad = render_tiles(
        jnp.moveaxis(slot_table[:, entry_idx], 0, 1), live_mask, anchor_x, anchor_y, target_images
    )
    slot_grad = (
        jnp.zeros((9, devices * columns), jnp.float32)
        .at[:, entry_idx]
        .add(jnp.moveaxis(feat_grad, 1, 0))
    )
    slot_grad = slot_grad.reshape(9, devices, columns)
    (raw_back,) = render_pull(slot_grad)
    raw_grad = give_back(raw_back)
    gradient = jnp.zeros(params.shape, jnp.float32).at[:, chosen].add(raw_grad)
    new_params, new_first, new_second = adam_step(params, first_moment, second_moment, gradient)
    return (shaded, new_params, new_first, new_second)


def solution(mesh):
    in_specs = (
        P(None, ("gauss", "render")),
        P(None, ("gauss", "render")),
        P(None, ("gauss", "render")),
        P(("gauss", "render"), None, None),
        P(("gauss", "render"), None),
        P(("gauss", "render"), None, None),
    )
    out_specs = (
        P(("gauss", "render"), None, None),
        P(None, ("gauss", "render")),
        P(None, ("gauss", "render")),
        P(None, ("gauss", "render")),
    )
    return jax.shard_map(
        per_device, mesh=mesh, in_specs=in_specs, out_specs=out_specs, check_vma=False
    )
```

profile of v0, /device:TPU:1, one launch (start us, length us, event | category | flops | bytes accessed | tf_op | source)
XLA Modules:
  0.0 939.6 jit_solution(16485924770003026470)
XLA Ops:
  2.9 54.4 %gather_fusion = f32[16384,59]{1,0:T(8,128)} fusion(f32[59,2048]{0,1:T(8,128)S(1)} %copy.278, s32[16384]{0:T(1024)S(1)} %broadcast_clamp_fusion.1), kind=kCustom, calls=%fused_computation | custom fusion | bytes 7798784 | tf_op jit(solution)/shard_map/gather | solution.py:246
  64.2 12.0 %all-to-all-start = ((f32[59,128,128]{2,0,1:T(8,128)}), f32[59,128,128]{2,0,1:T(8,128)}, u32[]{:S(2)}, u32[]{:S(2)}) async-start(f32[59,128,128]{2,0,1:T(8,128)} %bitcast.274), calls=%async_computation | async-start | bytes 8388608 | tf_op jit(solution)/shard_map/all_to_all | solution.py:229
  77.6 50.7 %all-to-all-done = f32[59,128,128]{2,0,1:T(8,128)} async-done(((f32[59,128,128]{2,0,1:T(8,128)}), f32[59,128,128]{2,0,1:T(8,128)}, u32[]{:S(2)}, u32[]{:S(2)}) %all-to-all-start) | async-done | bytes 3866656 | tf_op jit(solution)/shard_map/all_to_all | solution.py:229
  158.3 57.8 %gather_fusion.1 = f32[16384,9]{1,0:T(8,128)} fusion(f32[9,16384]{0,1:T(8,128)} %copy.339, s32[16384]{0:T(1024)S(1)} %broadcast_clamp_fusion), kind=kCustom, calls=%fused_computation.1 | custom fusion | bytes 1245184 | tf_op jit(solution)/shard_map/gather | solution.py:257
  221.3 392.6 %while.14 = (s32[]{:T(128)}, f32[8,4,3,256]{3,2,1,0:T(4,128)}, f32[8,4,9,512]{3,2,1,0:T(8,128)}, f32[8,4,9,512]{3,2,1,0:T(8,128)S(1)}, f32[8,4]{1,0:T(8,128)S(1)...) while((s32[]{:T(128)}, f32[8,4,3,256]{3,2,1,0:T(4,128)}, ...), condition=%wide.region_11.12_spmd, body=%wide.region_0.11_spmd.sunk | while | flops 247085056 | bytes 84722528 | solution.py:214
  244.8 9.6 %fusion.196 = f32[4,256,4,128]{1,2,3,0:T(4,128)S(1)} fusion(f32[4,256,4,128]{1,3,2,0:T(8,128)S(1)} %bitcast.272), kind=kOutput, calls=%fused_computation.73.clone.1 | output fusion | flops 66584576 | bytes 4194304 | tf_op jit(solution)/shard_map/reduce-window.14
  259.4 7.5 fusion.197
  293.8 9.6 %fusion.196 = f32[4,256,4,128]{1,2,3,0:T(4,128)S(1)} fusion(f32[4,256,4,128]{1,3,2,0:T(8,128)S(1)} %bitcast.272), kind=kOutput, calls=%fused_computation.73.clone.1 | output fusion | flops 66584576 | bytes 4194304 | tf_op jit(solution)/shard_map/reduce-window.14
  308.4 7.5 fusion.197
  342.8 9.6 %fusion.196 = f32[4,256,4,128]{1,2,3,0:T(4,128)S(1)} fusion(f32[4,256,4,128]{1,3,2,0:T(8,128)S(1)} %bitcast.272), kind=kOutput, calls=%fused_computation.73.clone.1 | output fusion | flops 66584576 | bytes 4194304 | tf_op jit(solution)/shard_map/reduce-window.14
  357.4 7.5 fusion.197
  391.8 9.6 %fusion.196 = f32[4,256,4,128]{1,2,3,0:T(4,128)S(1)} fusion(f32[4,256,4,128]{1,3,2,0:T(8,128)S(1)} %bitcast.272), kind=kOutput, calls=%fused_computation.73.clone.1 | output fusion | flops 66584576 | bytes 4194304 | tf_op jit(solution)/shard_map/reduce-window.14
  406.4 7.5 fusion.197
  440.8 9.6 %fusion.196 = f32[4,256,4,128]{1,2,3,0:T(4,128)S(1)} fusion(f32[4,256,4,128]{1,3,2,0:T(8,128)S(1)} %bitcast.272), kind=kOutput, calls=%fused_computation.73.clone.1 | output fusion | flops 66584576 | bytes 4194304 | tf_op jit(solution)/shard_map/reduce-window.14
  455.4 7.5 fusion.197
  489.8 9.6 %fusion.196 = f32[4,256,4,128]{1,2,3,0:T(4,128)S(1)} fusion(f32[4,256,4,128]{1,3,2,0:T(8,128)S(1)} %bitcast.272), kind=kOutput, calls=%fused_computation.73.clone.1 | output fusion | flops 66584576 | bytes 4194304 | tf_op jit(solution)/shard_map/reduce-window.14
  538.8 9.6 %fusion.196 = f32[4,256,4,128]{1,2,3,0:T(4,128)S(1)} fusion(f32[4,256,4,128]{1,3,2,0:T(8,128)S(1)} %bitcast.272), kind=kOutput, calls=%fused_computation.73.clone.1 | output fusion | flops 66584576 | bytes 4194304 | tf_op jit(solution)/shard_map/reduce-window.14
  553.4 7.5 fusion.197
  587.8 9.6 %fusion.196 = f32[4,256,4,128]{1,2,3,0:T(4,128)S(1)} fusion(f32[4,256,4,128]{1,3,2,0:T(8,128)S(1)} %bitcast.272), kind=kOutput, calls=%fused_computation.73.clone.1 | output fusion | flops 66584576 | bytes 4194304 | tf_op jit(solution)/shard_map/reduce-window.14
  602.4 7.5 fusion.197
  619.9 105.6 %scatter_custom_fusion = f32[9,16384]{0,1:T(8,128)} fusion(s32[16384]{0:T(1024)} %bitcast.366, f32[16384,9]{1,0:T(8,128)} %bitcast.277, f32[]{:T(128)} %constant.215.clone.1), kind=kCustom, calls=%fused_computation.145 | custom fusion | flops 147456 | bytes 590336 | tf_op jit(solution)/shard_map/scatter-add | solution.py:262
  725.5 50.7 %slice_reduce_fusion.8 = (f32[16384]{0:T(1024)S(1)}, f32[16384]{0:T(1024)S(1)}, f32[16384]{0:T(1024)S(1)}, f32[16384]{0:T(1024)S(1)}, f32[16384]{0:T(1024)S(1)},...) fusion(f32[9,16384]{0,1:T(8,128)} %scatter_custom_fusion), kind=kLoop, calls=%fused_computation.140 | loop fusion | bytes 1179648 | tf_op jit(solution)/shard_map/transpose(jvp())/unstack | solution.py:160
  791.1 51.4 %all-to-all-done.1 = f32[59,128,128]{2,0,1:T(8,128)} async-done(((f32[59,128,128]{2,0,1:T(8,128)}), f32[59,128,128]{2,0,1:T(8,128)}, u32[]{:S(2)}, u32[]{:S(2)}) %all-to-all-start.1) | async-done | bytes 3866656 | tf_op jit(solution)/shard_map/all_to_all | solution.py:234
  849.6 88.1 %scatter_custom_fusion.1 = f32[59,2048]{0,1:T(8,128)S(1)} fusion(s32[16384]{0:T(1024)S(1)} %fusion.104, f32[16384,59]{1,0:T(8,128)} %bitcast.276, f32[]{:T(128)} %constant.215.clone.1), kind=kCustom, calls=%fused_computation.158 | custom fusion | flops 966656 | bytes 483840 | tf_op jit(solution)/shard_map/scatter-add | solution.py:267
  (824 shorter events, 333.6 us)
Async XLA Ops:
  64.2 12.5 %copy-start.48 = (s32[32,512]{1,0:T(8,128)S(1)}, s32[32,512]{1,0:T(8,128)}, u32[]{:S(2)}) copy-start(s32[32,512]{1,0:T(8,128)} %param.13) | copy-start | bytes 196612
  64.2 12.6 %copy-start.56 = (f32[32,3,256]{2,0,1:T(8,128)S(1)}, f32[32,3,256]{2,0,1:T(8,128)}, u32[]{:S(2)}) copy-start(f32[32,3,256]{2,0,1:T(8,128)} %param.12) | copy-start | bytes 294916
  64.2 64.1 %all-to-all-start = ((f32[59,128,128]{2,0,1:T(8,128)}), f32[59,128,128]{2,0,1:T(8,128)}, u32[]{:S(2)}, u32[]{:S(2)}) async-start(f32[59,128,128]{2,0,1:T(8,128)} %bitcast.274), calls=%async_computation | async-start | bytes 8388608 | tf_op jit(solution)/shard_map/all_to_all | solution.py:229
  134.7 9.4 %copy-start.17 = (f32[1,128,128]{2,0,1:T(1,128)}, f32[1,128,128]{2,0,1:T(1,128)S(1)}, u32[]{:S(2)}) copy-start(f32[1,128,128]{2,0,1:T(1,128)S(1)} %get-tuple-element.269) | copy-start | bytes 196612
  134.7 9.4 %copy-start.19 = (f32[1,128,128]{2,0,1:T(1,128)}, f32[1,128,128]{2,0,1:T(1,128)S(1)}, u32[]{:S(2)}) copy-start(f32[1,128,128]{2,0,1:T(1,128)S(1)} %get-tuple-element.270) | copy-start | bytes 196612
  134.7 9.4 %copy-start.21 = (f32[1,128,128]{2,0,1:T(1,128)}, f32[1,128,128]{2,0,1:T(1,128)S(1)}, u32[]{:S(2)}) copy-start(f32[1,128,128]{2,0,1:T(1,128)S(1)} %get-tuple-element.271) | copy-start | bytes 196612
  134.8 9.4 %copy-start.23 = (f32[1,128,128]{2,0,1:T(1,128)}, f32[1,128,128]{2,0,1:T(1,128)S(1)}, u32[]{:S(2)}) copy-start(f32[1,128,128]{2,0,1:T(1,128)S(1)} %get-tuple-element.273) | copy-start | bytes 196612
  134.8 9.4 %copy-start.25 = (f32[1,128,128]{2,0,1:T(1,128)}, f32[1,128,128]{2,0,1:T(1,128)S(1)}, u32[]{:S(2)}) copy-start(f32[1,128,128]{2,0,1:T(1,128)S(1)} %get-tuple-element.274) | copy-start | bytes 196612
  134.8 9.4 %copy-start.27 = (f32[1,128,128]{2,0,1:T(1,128)}, f32[1,128,128]{2,0,1:T(1,128)S(1)}, u32[]{:S(2)}) copy-start(f32[1,128,128]{2,0,1:T(1,128)S(1)} %get-tuple-element.275) | copy-start | bytes 196612
  134.8 9.4 %copy-start.30 = (f32[1,128,128]{2,0,1:T(1,128)}, f32[1,128,128]{2,0,1:T(1,128)S(1)}, u32[]{:S(2)}) copy-start(f32[1,128,128]{2,0,1:T(1,128)S(1)} %get-tuple-element.268) | copy-start | bytes 196612
  134.8 9.4 %copy-start.42 = (f32[1,128,128]{2,0,1:T(1,128)}, f32[1,128,128]{2,0,1:T(1,128)S(1)}, u32[]{:S(2)}) copy-start(f32[1,128,128]{2,0,1:T(1,128)S(1)} %get-tuple-element.272) | copy-start | bytes 196612
  259.4 7.6 copy-start.1
  308.4 7.6 copy-start.1
  357.4 7.6 copy-start.1
  406.4 7.6 copy-start.1
  553.4 7.6 copy-start.1
  602.4 7.6 copy-start.1
  725.5 50.8 %copy-start.53 = (f32[1,128,128]{2,1,0:T(8,128)S(1)}, f32[1,128,128]{2,1,0:T(8,128)}, u32[]{:S(2)}) copy-start(f32[1,128,128]{2,1,0:T(8,128)} %get-tuple-element.185) | copy-start | bytes 196612
  725.5 51.0 %copy-start.52 = (f32[1,128,128]{2,1,0:T(8,128)S(1)}, f32[1,128,128]{2,1,0:T(8,128)}, u32[]{:S(2)}) copy-start(f32[1,128,128]{2,1,0:T(8,128)} %get-tuple-element.187) | copy-start | bytes 196612
  784.1 58.5 %all-to-all-start.1 = ((f32[59,128,128]{2,0,1:T(8,128)}), f32[59,128,128]{2,0,1:T(8,128)}, u32[]{:S(2)}, u32[]{:S(2)}) async-start(f32[59,128,128]{2,0,1:T(8,128)} %copy.344), calls=%async_computation.1 | async-start | bytes 8388608 | tf_op jit(solution)/shard_map/all_to_all | solution.py:234
  849.6 88.4 %copy-start.6 = (f32[59,2048]{1,0:T(8,128)S(1)}, f32[59,2048]{1,0:T(8,128)}, u32[]{:S(2)}) copy-start(f32[59,2048]{1,0:T(8,128)} %param.9) | copy-start | bytes 1449988
  849.6 88.4 %copy-start.44 = (f32[59,2048]{1,0:T(8,128)S(1)}, f32[59,2048]{1,0:T(8,128)}, u32[]{:S(2)}) copy-start(f32[59,2048]{1,0:T(8,128)} %param.10) | copy-start | bytes 1449988
  849.6 88.4 %copy-start.45 = (f32[59,2048]{1,0:T(8,128)S(1)}, f32[59,2048]{1,0:T(8,128)}, u32[]{:S(2)}) copy-start(f32[59,2048]{1,0:T(8,128)} %param.11) | copy-start | bytes 1449988
  849.6 88.5 %copy-start.61 = (f32[59]{0:T(128)S(1)}, f32[59]{0:T(128)}, u32[]{:S(2)}) copy-start(f32[59]{0:T(128)} %constant.258.clone) | copy-start | bytes 712
  (194 other events, 375.0 us)
where the time goes:
time: 948 us; the launch traced here: 940 us
  other arithmetic  436 us (46%)
  local copies, waits for them, and re-layouts  296 us (31%)
  waiting for transfers between devices  102 us (11%)
  matrix products  81.4 us (9%)
  starting transfers between devices  18.3 us (2%)
    another operation x48, other arithmetic  138 us
    scatter-add x1, other arithmetic, per_device(): slot_grad = jnp.zeros((9, devices * columns), jnp.float32).at[:, entry_id...  106 us
    scatter-add x1, other arithmetic, per_device(): gradient = jnp.zeros(params.shape, jnp.float32).at[:, chosen].add(raw_grad)  88.1 us
    dot_general x24, matrix products, composite(): jnp.einsum('dwo,doy->dwy', feature_vectors[:, 6:9, :], alpha_values * tra...  81.4 us
    gather x2, local copies, waits for them, and re-layouts, per_device(): outgoing = params[:, chosen]  61.3 us
    reduce_sum x8, other arithmetic, composite(): feature_vectors[:, 3, :, None] * delta_x * delta_y  59.6 us
    gather x1, local copies, waits for them, and re-layouts, per_device(): slot_table[:, entry_idx]  57.8 us
    another operation x3, local copies, waits for them, and re-layouts, project(): return jnp.stack(jnp.broadcast_arrays(*stacked))  56.3 us
  transfers between devices with their start and end apart: 2, of which 2 were waited for; matrix products, arithmetic and copies ran while one was open for 0% of the time, Pallas kernels for 0%

commit v1 on v0

v1 whole, which is shorter than its diff:
```python
import functools
import math

import jax
import jax.numpy as jnp
import numpy as np
from jax import lax
from jax.experimental import pallas as pl
from jax.experimental.pallas import tpu as pltpu
from jax.sharding import PartitionSpec as P

PARAMS = 59
PIX = 256
VIEWS = 16
LIST = 512
TILE_DEV = 32
GS_DEV = 2048
DEVICES = 128
CAP = 128
FEATS = 9
BLOCKS = 16
PROWS = 64
LANES = 128
SLABS = 4
LOG2E = 1.4426950408889634
AXES = ("gauss", "render")
VMEM_LIMIT = 56 * 1024 * 1024

sh_first = 0.28209479177387814
sh_second = 0.4886025119029199
sh_third = (
    1.0925484305920792,
    -1.0925484305920792,
    0.31539156525252005,
    -1.0925484305920792,
    0.5462742152960396,
)
sh_fourth = (
    -0.5900435899266435,
    2.890611442640554,
    -0.4570457994644658,
    0.3731763325901154,
    -0.4570457994644658,
    1.445305721320277,
    -0.5900435899266435,
)
tilt_reach = 0.25
beta_one = 0.9
beta_two = 0.999
adam_epsilon = 1e-15
adam_count = 1000.0


def rate_table():
    table = np.full((PARAMS,), 0.000125)
    table[0:3] = 0.0016
    table[3:6] = 0.005
    table[6:10] = 0.001
    table[10] = 0.05
    table[11] = 0.0025
    table[27] = 0.0025
    table[43] = 0.0025
    return np.broadcast_to(table.astype(np.float32)[:, None], (PARAMS, LANES))


def sh_basis(dir_x, dir_y, dir_z):
    sq_x = dir_x * dir_x
    sq_y = dir_y * dir_y
    sq_z = dir_z * dir_z
    return [
        sh_first,
        -sh_second * dir_y,
        sh_second * dir_z,
        -sh_second * dir_x,
        sh_third[0] * dir_x * dir_y,
        sh_third[1] * dir_y * dir_z,
        sh_third[2] * (2.0 * sq_z - sq_x - sq_y),
        sh_third[3] * dir_x * dir_z,
        sh_third[4] * (sq_x - sq_y),
        sh_fourth[0] * dir_y * (3.0 * sq_x - sq_y),
        sh_fourth[1] * dir_x * dir_y * dir_z,
        sh_fourth[2] * dir_y * (4.0 * sq_z - sq_x - sq_y),
        sh_fourth[3] * dir_z * (2.0 * sq_z - 3.0 * sq_x - 3.0 * sq_y),
        sh_fourth[4] * dir_x * (4.0 * sq_z - sq_x - sq_y),
        sh_fourth[5] * dir_z * (sq_x - sq_y),
        sh_fourth[6] * dir_x * (sq_x - 3.0 * sq_y),
    ]


def camera_constants(camera):
    angle = camera * (2.0 * math.pi / VIEWS)
    lean_x = tilt_reach * math.cos(angle)
    lean_y = tilt_reach * math.sin(angle)
    length = math.sqrt(1.0 + lean_x * lean_x + lean_y * lean_y)
    basis = sh_basis(lean_x / length, lean_y / length, -1.0 / length)
    return (lean_x, lean_y, 16.0 * (camera % 4), 16.0 * (camera // 4), basis)


CAMERAS = [camera_constants(camera) for camera in range(VIEWS)]


def spread(log_scales, quat):
    squares = [jnp.exp(2.0 * value) for value in log_scales]
    norm = jnp.sqrt(quat[0] * quat[0] + quat[1] * quat[1] + quat[2] * quat[2] + quat[3] * quat[3])
    q_w, q_x, q_y, q_z = [part / norm for part in quat]
    rotation = [
        [
            1.0 - 2.0 * (q_y * q_y + q_z * q_z),
            2.0 * (q_x * q_y - q_w * q_z),
            2.0 * (q_x * q_z + q_w * q_y),
        ],
        [
            2.0 * (q_x * q_y + q_w * q_z),
            1.0 - 2.0 * (q_x * q_x + q_z * q_z),
            2.0 * (q_y * q_z - q_w * q_x),
        ],
        [
            2.0 * (q_x * q_z - q_w * q_y),
            2.0 * (q_y * q_z + q_w * q_x),
            1.0 - 2.0 * (q_x * q_x + q_y * q_y),
        ],
    ]
    return [
        rotation[row][0] * rotation[col][0] * squares[0]
        + rotation[row][1] * rotation[col][1] * squares[1]
        + rotation[row][2] * rotation[col][2] * squares[2]
        for row, col in ((0, 0), (0, 1), (0, 2), (1, 1), (1, 2), (2, 2))
    ]


def conic_of(sigma, lean_x, lean_y):
    s_xx, s_xy, s_xz, s_yy, s_yz, s_zz = sigma
    cov_xx = s_xx + (2.0 * lean_x) * s_xz + (lean_x * lean_x) * s_zz + 0.3
    cov_xy = s_xy + lean_x * s_yz + lean_y * s_xz + (lean_x * lean_y) * s_zz
    cov_yy = s_yy + (2.0 * lean_y) * s_yz + (lean_y * lean_y) * s_zz + 0.3
    inverse = 1.0 / (cov_xx * cov_yy - cov_xy * cov_xy)
    return cov_yy * inverse, -cov_xy * inverse, cov_xx * inverse


def raw_colour(row, basis, channel):
    total = 0.5 + row(11 + 16 * channel) * basis[0]
    for term in range(1, 16):
        total = total + row(11 + 16 * channel + term) * basis[term]
    return total


def block_rows(source, dest):
    rows = source.shape[0]
    for block in range(BLOCKS):
        dest[pl.ds(block * PROWS, rows), :] = source[:, pl.ds(block * LANES, LANES)]


def strided(ref, row):
    return ref[pl.ds(row, BLOCKS, stride=PROWS), :]


def parts_of(value, count):
    parts = []
    for step in range(count):
        part = value.astype(jnp.bfloat16)
        parts.append(part)
        if step + 1 < count:
            value = value - part.astype(jnp.float32)
    return parts


def project_kernel(params_ref, index_ref, out_ref, rows_ref, table_ref):
    block_rows(params_ref, rows_ref)
    row = functools.partial(strided, rows_ref)
    sigma = spread([row(3 + k) for k in range(3)], [row(6 + k) for k in range(4)])
    logit = row(10)
    log_opacity = -LOG2E * (jnp.maximum(-logit, 0.0) + jnp.log1p(jnp.exp(-jnp.abs(logit))))
    for camera in range(VIEWS):
        lean_x, lean_y, shift_x, shift_y, basis = CAMERAS[camera]
        height = row(2)
        features = [row(0) + lean_x * height - shift_x, row(1) + lean_y * height - shift_y]
        features += list(conic_of(sigma, lean_x, lean_y))
        features.append(log_opacity)
        features += [jnp.maximum(raw_colour(row, basis, k), 0.0) for k in range(3)]
        for f in range(FEATS):
            table_ref[pl.ds((camera * FEATS + f) * BLOCKS, BLOCKS), :] = features[f]

    @pl.loop(0, VIEWS)
    def _(camera):
        chosen = index_ref[pl.ds(pl.multiple_of(camera * 8, 8), 8), :]
        low = jnp.bitwise_and(chosen, LANES - 1)
        high = jnp.right_shift(chosen, 7)
        totals = [jnp.zeros((8, LANES), jnp.float32) for _ in range(FEATS)]
        for block in range(BLOCKS):
            here = high == block
            for f in range(FEATS):
                line = table_ref[pl.ds((camera * FEATS + f) * BLOCKS + block, 1), :]
                line = jnp.broadcast_to(line, (8, LANES))
                picked = jnp.take_along_axis(line, low, axis=1)
                totals[f] = jnp.where(here, picked, totals[f])
        for f in range(FEATS):
            out_ref[pl.ds(camera * 8 * FEATS + f, 8, stride=FEATS), :] = totals[f]


def invert_kernel(list_ref, lane_ref, row_ref):
    sublane = lax.broadcasted_iota(jnp.int32, (LANES, LANES), 0)
    lane = lax.broadcasted_iota(jnp.int32, (LANES, LANES), 1).astype(jnp.float32)

    def step(pair, total):
        owners, slots = [], []
        for member in range(2):
            line = list_ref[pl.ds(pair * 2 + member, 1), :]
            low = jnp.broadcast_to(jnp.bitwise_and(line, CAP - 1), (LANES, LANES))
            high = jnp.broadcast_to(jnp.right_shift(line, 7), (LANES, LANES))
            number = (pair * 2 + member + 1).astype(jnp.float32)
            owners.append(jnp.where(high == sublane, 1.0, 0.0).astype(jnp.bfloat16))
            same = low == sublane
            slots.append(
                jnp.concatenate([jnp.where(same, lane, 0.0), jnp.where(same, number, 0.0)], 0).astype(
                    jnp.bfloat16
                )
            )
        return total + lax.dot_general(
            jnp.concatenate(owners, 1),
            jnp.concatenate(slots, 1),
            (((1,), (1,)), ((), ())),
            preferred_element_type=jnp.float32,
        )

    total = lax.fori_loop(0, LANES // 2, step, jnp.zeros((LANES, 2 * LANES), jnp.float32), unroll=4)
    lane_ref[...] = total[:, :LANES].astype(jnp.int32)
    row_ref[...] = total[:, LANES:].astype(jnp.int32) - 1


def lane_gather(table, stride_row, stride_feature, low, high, store):
    spans = len(low)

    def step(source, totals):
        totals = list(totals)
        here = [h == source for h in high]
        for f in range(FEATS):
            line = table[pl.ds(source * stride_row + f * stride_feature, 1), :]
            line = jnp.broadcast_to(line, (8, LANES))
            for u in range(spans):
                picked = jnp.take_along_axis(line, low[u], axis=1)
                totals[f * spans + u] = jnp.where(here[u], picked, totals[f * spans + u])
        return tuple(totals)

    blank = tuple(jnp.zeros((8, LANES), jnp.float32) for _ in range(FEATS * spans))
    totals = lax.fori_loop(0, LANES, step, blank, unroll=16)
    for f in range(FEATS):
        for u in range(spans):
            store(f, u, totals[f * spans + u])


KROWS = 32
GRADS = 16
GROUP_ROWS = LIST * 8


def render_kernel(
    table_ref,
    list_ref,
    lane_ref,
    row_ref,
    target_ref,
    expand_ref,
    mono_ref,
    image_ref,
    back_ref,
    feat_ref,
    coef_ref,
    alpha_ref,
    weight_ref,
    colour_ref,
    push_ref,
    grad_ref,
    moment_ref,
):
    render = lax.axis_index(AXES[1])
    device = lax.axis_index(AXES[0]) * lax.axis_size(AXES[1]) + render
    strip = lax.rem(device, DEVICES // VIEWS)
    lane_tile = jnp.bitwise_and(lax.broadcasted_iota(jnp.int32, (8, LANES), 1), 7)
    centre_x = 16.0 * lane_tile.astype(jnp.float32) + 8.0

    @pl.loop(0, 8)
    def _(part):
        spans = [pl.ds(pl.multiple_of(part * 16 + u * 8, 8), 8) for u in range(2)]
        entries = [list_ref[span, :] for span in spans]
        low = [jnp.bitwise_and(entry, CAP - 1) for entry in entries]
        high = [jnp.right_shift(entry, 7) for entry in entries]

        def store(f, u, value):
            feat_ref[pl.ds(pl.multiple_of(f * LANES + part * 16 + u * 8, 8), 8), :] = value

        lane_gather(table_ref, FEATS, 1, low, high, store)

    zero = jnp.zeros((8, LANES), jnp.float32)

    @pl.loop(0, 16)
    def _(octet):
        base = pl.multiple_of(octet * 8, 8)
        feature = [feat_ref[pl.ds(pl.multiple_of(f * LANES + octet * 8, 8), 8), :] for f in range(FEATS)]
        live = list_ref[pl.ds(base, 8), :] >= 0
        centre_y = (16 * (strip * SLABS + octet // 4) + 8).astype(jnp.float32)
        m_x = feature[0] - centre_x
        m_y = feature[1] - centre_y
        a = (-0.5 * LOG2E) * feature[2]
        b = -LOG2E * feature[3]
        c = (-0.5 * LOG2E) * feature[4]
        to_x = 2.0 * a * m_x + b * m_y
        to_y = b * m_x + 2.0 * c * m_y
        level = a * m_x * m_x + b * m_x * m_y + c * m_y * m_y
        level = jnp.where(live, level + feature[5], -10000.0)
        values = [a, b, c, -to_x, -to_y, level] + feature[6:9]
        place = 0
        for value in values:
            for part in parts_of(value, 3):
                coef_ref[pl.ds(octet * 8 * KROWS + place, 8, stride=KROWS), :] = part.astype(jnp.float32)
                place += 1
        for rest in range(place, KROWS):
            coef_ref[pl.ds(octet * 8 * KROWS + rest, 8, stride=KROWS), :] = zero

    diagonal = lax.broadcasted_iota(jnp.int32, (8, LANES), 0) == lane_tile

    @pl.loop(0, SLABS)
    def _(group):
        @pl.loop(0, 32, unroll=2)
        def _(line):
            start = pl.multiple_of((group * 32 + line) * KROWS, KROWS)
            left = coef_ref[pl.ds(start, KROWS), :].T.astype(jnp.bfloat16)
            wide = jnp.dot(left, expand_ref[...], preferred_element_type=jnp.float32)
            out = pl.ds(pl.multiple_of(line * LANES, LANES), LANES)
            alpha_ref[out, :] = wide[:, :PIX]
            colour_ref[out, :] = wide[:, PIX:]

        def forward(block, carry):
            through = list(carry[:2])
            image = list(carry[2:])
            for u in range(16):
                here = pl.ds(pl.multiple_of(block * LANES + u * 8, 8), 8)
                shade = [colour_ref[here, pl.ds(k * LANES, LANES)] for k in range(3)]
                for half in range(2):
                    cols = pl.ds(half * LANES, LANES)
                    alpha = jnp.minimum(jnp.exp2(alpha_ref[here, cols]), 0.99)
                    weight = alpha * through[half]
                    through[half] = through[half] * (1.0 - alpha)
                    alpha_ref[here, cols] = alpha
                    weight_ref[here, cols] = weight
                    for k in range(3):
                        image[k * 2 + half] = image[k * 2 + half] + shade[k] * weight
            return tuple(through + image)

        ones = jnp.ones((8, LANES), jnp.float32)
        image = lax.fori_loop(0, 32, forward, (ones, ones) + (zero,) * 6)[2:]
        residual = []
        tiles = pl.ds(pl.multiple_of(group * 8, 8), 8)
        for k in range(3):
            for half in range(2):
                cols = pl.ds(k * PIX + half * LANES, LANES)
                image_ref[tiles, cols] = image[k * 2 + half]
                residual.append(image[k * 2 + half] - target_ref[tiles, cols])

        def backward(count, carry):
            behind = list(carry)
            block = 31 - count
            for pair in range(7, -1, -1):
                pushes = [[None, None], [None, None]]
                for member in (1, 0):
                    here = pl.ds(pl.multiple_of(block * LANES + pair * 16 + member * 8, 8), 8)
                    shade = [colour_ref[here, pl.ds(k * LANES, LANES)] for k in range(3)]
                    for half in range(2):
                        cols = pl.ds(half * LANES, LANES)
                        alpha = alpha_ref[here, cols]
                        weight = weight_ref[here, cols]
                        worth = (
                            shade[0] * residual[half]
                            + shade[1] * residual[2 + half]
                            + shade[2] * residual[4 + half]
                        )
                        gain = worth - behind[half]
                        behind[half] = behind[half] + alpha * gain
                        pushes[half][member] = jnp.where(alpha < 0.99, weight * gain, 0.0)
                rows = pl.ds(pl.multiple_of(block * LANES + pair * 16, 16), 16)
                for half in range(2):
                    value = jnp.concatenate(pushes[half], 0)
                    for which, part in enumerate(parts_of(value, 2)):
                        push_ref[which, rows, pl.ds(half * LANES, LANES)] = part
            return tuple(behind)

        lax.fori_loop(0, 32, backward, (zero, zero))
        stack = jnp.concatenate(
            [jnp.concatenate([residual[k * 2], residual[k * 2 + 1]], 1) for k in range(3)], 0
        )
        stack = jnp.concatenate(parts_of(stack, 2), 0)
        contract = (((1,), (1,)), ((), ()))

        @pl.loop(0, 8)
        def _(chunk):
            rows = pl.ds(pl.multiple_of(chunk * 512, 512), 512)
            moments = lax.dot_general(
                mono_ref[...], push_ref[0, rows, :], contract, preferred_element_type=jnp.float32
            ) + lax.dot_general(
                mono_ref[...], push_ref[1, rows, :], contract, preferred_element_type=jnp.float32
            )
            tints = 0.0
            for part in parts_of(weight_ref[rows, :], 2):
                tints = tints + lax.dot_general(stack, part, contract, preferred_element_type=jnp.float32)
            tints = tints[:24] + tints[24:]
            for line in range(4):
                cols = slice(line * LANES, (line + 1) * LANES)
                base = ((group * 32) + chunk * 4 + line) * GRADS
                moment_ref[pl.ds(pl.multiple_of(base, 8), 8), :] = moments[:8, cols]
                for k in range(3):
                    own = jnp.where(diagonal, tints[k * 8 : k * 8 + 8, cols], 0.0)
                    moment_ref[pl.ds(base + 8 + k, 1), :] = jnp.sum(own, 0, keepdims=True)

    @pl.loop(0, 16)
    def _(octet):
        feature = [feat_ref[pl.ds(pl.multiple_of(f * LANES + octet * 8, 8), 8), :] for f in range(5)]
        centre_y = (16 * (strip * SLABS + octet // 4) + 8).astype(jnp.float32)
        m_x = feature[0] - centre_x
        m_y = feature[1] - centre_y

        def moment(k):
            return moment_ref[pl.ds(octet * 8 * GRADS + k, 8, stride=GRADS), :]

        total, s_x, s_y, s_xx, s_xy, s_yy = [moment(k) for k in range(6)]
        along_x = s_x - m_x * total
        along_y = s_y - m_y * total
        results = [
            feature[2] * along_x + feature[3] * along_y,
            feature[3] * along_x + feature[4] * along_y,
            -0.5 * (s_xx - m_x * (s_x + along_x)),
            -(s_xy - m_x * s_y - m_y * along_x),
            -0.5 * (s_yy - m_y * (s_y + along_y)),
            total,
            moment(8),
            moment(9),
            moment(10),
        ]
        for f in range(FEATS):
            grad_ref[pl.ds(pl.multiple_of(f * LANES + octet * 8, 8), 8), :] = results[f]

    @pl.loop(0, 8)
    def _(part):
        spans = [pl.ds(pl.multiple_of(part * 16 + u * 8, 8), 8) for u in range(2)]
        low = [lane_ref[span, :] for span in spans]
        high = [row_ref[span, :] for span in spans]

        def store(f, u, value):
            back_ref[pl.ds((part * 16 + u * 8) * FEATS + f, 8, stride=FEATS), :] = value

        lane_gather(grad_ref, 1, LANES, low, high, store)


SUM_PARTS = 2


def update_kernel(
    back_ref, index_ref, params_ref, first_ref, second_ref, rate_ref,
    new_params_ref, new_first_ref, new_second_ref,
    rows_ref, sums_ref, slope_ref, tint_ref,
):
    block_rows(params_ref, rows_ref)
    row = functools.partial(strided, rows_ref)
    sublane = lax.broadcasted_iota(jnp.int32, (LANES, LANES), 0)
    short = lax.broadcasted_iota(jnp.int32, (BLOCKS, LANES), 0)

    @pl.loop(0, VIEWS)
    def _(camera):
        total = jnp.zeros((SUM_PARTS * FEATS * BLOCKS, LANES), jnp.float32)
        for pair in range(4):
            places, values = [], []
            for member in range(2):
                renderer = camera * 8 + pair * 2 + member
                line = index_ref[pl.ds(renderer, 1), :]
                low = jnp.broadcast_to(jnp.bitwise_and(line, LANES - 1), (LANES, LANES))
                high = jnp.broadcast_to(jnp.right_shift(line, 7), (BLOCKS, LANES))
                places.append(jnp.where(low == sublane, 1.0, 0.0).astype(jnp.bfloat16))
                here = high == short
                stacks = []
                for f in range(FEATS):
                    value = jnp.broadcast_to(back_ref[pl.ds(renderer * FEATS + f, 1), :], (BLOCKS, LANES))
                    stacks.append(jnp.where(here, value, 0.0))
                stack = jnp.concatenate(stacks, 0)
                values.append(jnp.concatenate(parts_of(stack, SUM_PARTS), 0))
            total = total + lax.dot_general(
                jnp.concatenate(values, 1),
                jnp.concatenate(places, 1),
                (((1,), (1,)), ((), ())),
                preferred_element_type=jnp.float32,
            )
        size = FEATS * BLOCKS
        merged = total[:size]
        for part in range(1, SUM_PARTS):
            merged = merged + total[part * size : (part + 1) * size]
        sums_ref[pl.ds(pl.multiple_of(camera * size, size), size), :] = merged

    logs = [row(3 + k) for k in range(3)]
    quat = [row(6 + k) for k in range(4)]
    sigma, spread_pull = jax.vjp(spread, logs, quat)
    blank = jnp.zeros((BLOCKS, LANES), jnp.float32)
    d_sigma = [blank] * 6
    d_x, d_y, d_z, d_log = blank, blank, blank, blank
    for camera in range(VIEWS):
        lean_x, lean_y, _, _, basis = CAMERAS[camera]

        def pushed(f):
            return sums_ref[pl.ds((camera * FEATS + f) * BLOCKS, BLOCKS), :]

        d_x = d_x + pushed(0)
        d_y = d_y + pushed(1)
        d_z = d_z + lean_x * pushed(0) + lean_y * pushed(1)
        _, pull = jax.vjp(lambda values: conic_of(values, lean_x, lean_y), sigma)
        (more,) = pull((pushed(2), pushed(3), pushed(4)))
        d_sigma = [old + new for old, new in zip(d_sigma, more)]
        d_log = d_log + pushed(5)
        for k in range(3):
            raw = raw_colour(row, basis, k)
            gate = jnp.where(raw > 0.0, 1.0, jnp.where(raw == 0.0, 0.5, 0.0))
            tint_ref[pl.ds((k * VIEWS + camera) * BLOCKS, BLOCKS), :] = gate * pushed(6 + k)
    d_scale, d_quat = spread_pull(d_sigma)
    slopes = [d_x, d_y, d_z] + list(d_scale) + list(d_quat) + [d_log / (1.0 + jnp.exp(row(10)))]
    for number, slope in enumerate(slopes):
        slope_ref[pl.ds(number, BLOCKS, stride=PROWS), :] = slope
    for k in range(3):
        for term in range(16):
            slope = blank
            for camera in range(VIEWS):
                tint = tint_ref[pl.ds((k * VIEWS + camera) * BLOCKS, BLOCKS), :]
                slope = slope + CAMERAS[camera][4][term] * tint
            slope_ref[pl.ds(11 + 16 * k + term, BLOCKS, stride=PROWS), :] = slope
    rates = rate_ref[...]
    for block in range(BLOCKS):
        cols = pl.ds(block * LANES, LANES)
        slope = slope_ref[pl.ds(block * PROWS, PARAMS), :]
        new_first = beta_one * first_ref[:, cols] + (1.0 - beta_one) * slope
        new_second = beta_two * second_ref[:, cols] + (1.0 - beta_two) * slope * slope
        first_hat = new_first / (1.0 - beta_one**adam_count)
        second_hat = new_second / (1.0 - beta_two**adam_count)
        new_first_ref[:, cols] = new_first
        new_second_ref[:, cols] = new_second
        new_params_ref[:, cols] = params_ref[:, cols] - rates * first_hat / (
            jnp.sqrt(second_hat) + adam_epsilon
        )


WHOLE = pl.BlockSpec(memory_space=pltpu.VMEM)


def run_kernel(kernel, shapes, scratch, *operands):
    many = isinstance(shapes, list)
    return pl.pallas_call(
        kernel,
        out_shape=shapes,
        in_specs=[WHOLE] * len(operands),
        out_specs=[WHOLE] * len(shapes) if many else WHOLE,
        scratch_shapes=scratch,
        compiler_params=pltpu.CompilerParams(vmem_limit_bytes=VMEM_LIMIT),
    )(*operands)


def table(rows, dtype=jnp.float32):
    return jax.ShapeDtypeStruct((rows, LANES), dtype)


def buffer(*shape, dtype=jnp.float32):
    return pltpu.VMEM(shape, dtype)


def expand_table():
    x = np.arange(PIX) % 16 - 7.5
    y = np.arange(PIX) // 16 - 7.5
    wide = np.zeros((KROWS, PIX + 3 * LANES), np.float32)
    for number, mono in enumerate((x * x, x * y, y * y, x, y, np.ones(PIX))):
        wide[3 * number : 3 * number + 3, :PIX] = mono
    for k in range(3):
        wide[18 + 3 * k : 21 + 3 * k, PIX + k * LANES : PIX + (k + 1) * LANES] = 1.0
    narrow = np.zeros((16, PIX), np.float32)
    for number, mono in enumerate((np.ones(PIX), x, y, x * x, x * y, y * y)):
        narrow[number] = mono
    return jnp.asarray(wide, jnp.bfloat16), jnp.asarray(narrow, jnp.bfloat16)


def owner_features(params, index):
    return run_kernel(
        project_kernel,
        table(DEVICES * FEATS),
        [buffer(BLOCKS * PROWS, LANES), buffer(VIEWS * FEATS * BLOCKS, LANES)],
        params,
        index,
    )


def ordered(tile_lists):
    return tile_lists.reshape(SLABS, 8, LIST).transpose(0, 2, 1).reshape(LANES, LANES)


def inverse_lists(entries):
    return run_kernel(invert_kernel, [table(LANES, jnp.int32)] * 2, [], entries)


def render(received, entries, lanes, rows, target):
    wide, narrow = expand_table()
    return run_kernel(
        render_kernel,
        [jax.ShapeDtypeStruct((TILE_DEV, 3 * PIX), jnp.float32), table(DEVICES * FEATS)],
        [
            buffer(FEATS * LANES, LANES),
            buffer(LANES * KROWS, LANES),
            buffer(GROUP_ROWS, PIX),
            buffer(GROUP_ROWS, PIX),
            buffer(GROUP_ROWS, 3 * LANES),
            buffer(2, GROUP_ROWS, PIX, dtype=jnp.bfloat16),
            buffer(FEATS * LANES, LANES),
            buffer(LANES * GRADS, LANES),
        ],
        received,
        entries,
        lanes,
        rows,
        target,
        wide,
        narrow,
    )


def owner_update(back, index, params, first, second):
    shape = jax.ShapeDtypeStruct(params.shape, jnp.float32)
    return run_kernel(
        update_kernel,
        [shape] * 3,
        [
            buffer(BLOCKS * PROWS, LANES),
            buffer(VIEWS * FEATS * BLOCKS, LANES),
            buffer(BLOCKS * PROWS, LANES),
            buffer(3 * VIEWS * BLOCKS, LANES),
        ],
        back,
        index,
        params,
        first,
        second,
        jnp.asarray(rate_table()),
    )


def exchange(values):
    chunks = values.reshape(DEVICES, 1, FEATS * LANES)
    arrived = lax.all_to_all(chunks, AXES, split_axis=0, concat_axis=0, tiled=True)
    return arrived.reshape(DEVICES * FEATS, LANES)


def per_device(params, first_moment, second_moment, target_images, tile_lists, send_index):
    index = send_index[0]
    outgoing = owner_features(params, index)
    entries = ordered(tile_lists)
    received = exchange(outgoing)
    lanes, rows = inverse_lists(entries)
    target = target_images.reshape(TILE_DEV, 3 * PIX)
    image, returning = render(received, entries, lanes, rows, target)
    back = exchange(returning)
    new_params, new_first, new_second = owner_update(back, index, params, first_moment, second_moment)
    return (image.reshape(target_images.shape), new_params, new_first, new_second)


def solution(mesh):
    in_specs = (
        P(None, AXES),
        P(None, AXES),
        P(None, AXES),
        P(AXES, None, None),
        P(AXES, None),
        P(AXES, None, None),
    )
    out_specs = (P(AXES, None, None), P(None, AXES), P(None, AXES), P(None, AXES))
    return jax.shard_map(
        per_device, mesh=mesh, in_specs=in_specs, out_specs=out_specs, check_vma=False
    )
```

time: 948 us -> 187 us (0.20)
  other arithmetic: 436 us -> 0 us
  local copies, waits for them, and re-layouts: 296 us -> 4.56 us
  Pallas kernels: 0 us -> 146 us
  waiting for transfers between devices: 102 us -> 18.6 us
  matrix products: 81.4 us -> 0 us
    scatter-add x2 -> x0, other arithmetic: 194 us -> none  [the longest x1 106 us: per_device(): slot_grad = jnp.zeros((9, devices * columns), jnp.float32).at[:, entry_id...]
    pallas_call x0 -> x4, Pallas kernels: none -> 146 us  [run_kernel(): pl.pallas_call(kernel, out_shape=shapes, in_specs=[WHOLE] * len(operands)...]
    another operation x48 -> x0, other arithmetic: 138 us -> none
    gather x3 -> x0, local copies, waits for them, and re-layouts: 119 us -> none  [the longest x2 61.3 us: per_device(): outgoing = params[:, chosen]]
    all_to_all x2, waiting for transfers between devices: 102 us -> 18.6 us  [exchange(): lax.all_to_all(chunks, AXES, split_axis=0, concat_axis=0, tiled=True)]
    dot_general x24 -> x0, matrix products: 81.4 us -> none  [composite(): jnp.einsum('dwo,doy->dwy', feature_vectors[:, 6:9, :], alpha_values * tra...]
    another operation x51 -> x1, local copies, waits for them, and re-layouts: 62.5 us -> 0.8 us  [the longest x3 56.3 us: project(): return jnp.stack(jnp.broadcast_arrays(*stacked))]
    reduce_sum x8 -> x0, other arithmetic: 59.6 us -> none  [composite(): feature_vectors[:, 3, :, None] * delta_x * delta_y]
  transfers between devices with their start and end apart: 2 -> 2, of which waited for: 2 -> 2; matrix products, arithmetic and copies ran while one was open for 0% -> 1% of each run, Pallas kernels for 0% -> 4%
where the time goes in v1:
time: 187 us
  Pallas kernels  146 us (78%)
  waiting for transfers between devices  18.6 us (10%)
  starting transfers between devices  16.3 us (9%)
  local copies, waits for them, and re-layouts  4.56 us (2%)
    pallas_call x4, Pallas kernels, run_kernel(): pl.pallas_call(kernel, out_shape=shapes, in_specs=[WHOLE] * len(operands)...  146 us
    all_to_all x2, waiting for transfers between devices, exchange(): lax.all_to_all(chunks, AXES, split_axis=0, concat_axis=0, tiled=True)  18.6 us
    all_to_all x2, starting transfers between devices, exchange(): lax.all_to_all(chunks, AXES, split_axis=0, concat_axis=0, tiled=True)  16.3 us
  transfers between devices with their start and end apart: 2, of which 2 were waited for; matrix products, arithmetic and copies ran while one was open for 1% of the time, Pallas kernels for 4%

profile of v1, /device:TPU:1, one launch (start us, length us, event | category | flops | bytes accessed | tf_op | source)
XLA Modules:
  0.0 186.5 jit_solution(418275219927090936)
XLA Ops:
  0.6 9.5 %shard_map.120 = f32[1152,128]{1,0:T(8,128)} custom-call(f32[59,2048]{1,0:T(8,128)} %params_ref.3, s32[128,128]{1,0:T(8,128)} %bitcast.19), custom_call_target="tpu_custom_call" | custom-call | tf_op jit(solution)/shard_map/pallas_call | solution.py:549
  10.1 0.0 copy-start.2
  10.1 11.5 %all-to-all-start = ((f32[128,1,1152]{2,1,0:T(1,128)}), f32[128,1,1152]{2,1,0:T(1,128)S(1)}, u32[]{:S(2)}, u32[]{:S(2)}) async-start(f32[128,1,1152]{2,1,0:T(1,128)} %bitcast.15), calls=%async_computation | async-start | bytes 1179648 | tf_op jit(solution)/shard_map/all_to_all | solution.py:646
  21.6 0.0 copy-done.2
  21.6 0.0 copy-start.4
  21.7 0.6 copy.25
  22.3 0.2 copy-done.4
  22.5 0.3 copy.20
  22.8 1.1 reshape.35.list_ref
  23.9 6.8 %shard_map.121 = (s32[128,128]{1,0:T(8,128)}, s32[128,128]{1,0:T(8,128)}) custom-call(s32[128,128]{1,0:T(8,128)} %reshape.35.list_ref), custom_call_target="tpu_custom_call" | custom-call | tf_op jit(solution)/shard_map/pallas_call | solution.py:549
  30.7 5.0 %all-to-all-done = f32[128,1,1152]{2,1,0:T(1,128)S(1)} async-done(((f32[128,1,1152]{2,1,0:T(1,128)}), f32[128,1,1152]{2,1,0:T(1,128)S(1)}, u32[]{:S(2)}, u32[]{:S(2)}) %all-to-all-start) | async-done | bytes 589856 | tf_op jit(solution)/shard_map/all_to_all | solution.py:646
  35.7 0.0 copy-start
  35.7 0.8 copy-done
  36.5 117.0 %shard_map.122 = (f32[32,768]{1,0:T(8,128)}, f32[1152,128]{1,0:T(8,128)}) custom-call(f32[1152,128]{1,0:T(8,128)} %bitcast.14, s32[128,128]{1,0:T(8,128)} %reshape.35.list_ref, s32[128,128]{1,0:T(8,128)} %get-tuple-element.11.lane_ref, s32[128,128]{1,0:T(8,128)} %get-tuple-element.12.row_ref, f32[32,768]{1,0:T(8,128)} %bitcast.18, ...), custom_call_target="tpu_custom_call" | custom-call | tf_op jit(solution)/shard_map/pallas_call | solution.py:549
  153.5 0.0 copy-start.3
  153.5 4.8 %all-to-all-start.1 = ((f32[128,1,1152]{2,1,0:T(1,128)}), f32[128,1,1152]{2,1,0:T(1,128)S(1)}, u32[]{:S(2)}, u32[]{:S(2)}) async-start(f32[128,1,1152]{2,1,0:T(1,128)} %bitcast.17), calls=%async_computation.1 | async-start | bytes 1179648 | tf_op jit(solution)/shard_map/all_to_all | solution.py:646
  158.4 0.0 copy-done.3
  158.4 0.6 copy.27
  159.0 13.5 %all-to-all-done.1 = f32[128,1,1152]{2,1,0:T(1,128)S(1)} async-done(((f32[128,1,1152]{2,1,0:T(1,128)}), f32[128,1,1152]{2,1,0:T(1,128)S(1)}, u32[]{:S(2)}, u32[]{:S(2)}) %all-to-all-start.1) | async-done | bytes 589856 | tf_op jit(solution)/shard_map/all_to_all | solution.py:646
  172.6 0.0 copy-start.1
  172.6 0.0 copy-done.5
  172.6 0.8 jit_solution_.3.rate_ref
  173.4 0.0 copy-done.1
  173.4 13.1 %shard_map.123 = (f32[59,2048]{1,0:T(8,128)}, f32[59,2048]{1,0:T(8,128)}, f32[59,2048]{1,0:T(8,128)}) custom-call(f32[1152,128]{1,0:T(8,128)} %bitcast.16, s32[128,128]{1,0:T(8,128)} %bitcast.20, f32[59,2048]{1,0:T(8,128)} %params_ref.3, f32[59,2048]{1,0:T(8,128)} %first_ref.1, f32[59,2048]{1,0:T(8,128)} %second_ref.1, f32[59,128]{1,0:T(8,128)} %jit_solution_.3.rate_ref), custom_call_target="tpu_custom_call" | custom-call | tf_op jit(solution)/shard_map/pallas_call | solution.py:549
  (1 shorter events, 0.0 us)
Async XLA Ops:
  10.1 11.5 %copy-start.2 = (f32[32,3,256]{2,0,1:T(8,128)S(1)}, f32[32,3,256]{2,0,1:T(8,128)}, u32[]{:S(2)}) copy-start(f32[32,3,256]{2,0,1:T(8,128)} %param.12) | copy-start | bytes 294916
  10.1 25.6 %all-to-all-start = ((f32[128,1,1152]{2,1,0:T(1,128)}), f32[128,1,1152]{2,1,0:T(1,128)S(1)}, u32[]{:S(2)}, u32[]{:S(2)}) async-start(f32[128,1,1152]{2,1,0:T(1,128)} %bitcast.15), calls=%async_computation | async-start | bytes 1179648 | tf_op jit(solution)/shard_map/all_to_all | solution.py:646
  21.6 0.8 copy-start.4
  35.7 0.8 copy-start
  153.5 4.9 %copy-start.3 = (f32[32,768]{1,0:T(8,128)S(1)}, f32[32,768]{1,0:T(8,128)}, u32[]{:S(2)}) copy-start(f32[32,768]{1,0:T(8,128)} %get-tuple-element.13) | copy-start | bytes 294916
  153.5 19.0 %all-to-all-start.1 = ((f32[128,1,1152]{2,1,0:T(1,128)}), f32[128,1,1152]{2,1,0:T(1,128)S(1)}, u32[]{:S(2)}, u32[]{:S(2)}) async-start(f32[128,1,1152]{2,1,0:T(1,128)} %bitcast.17), calls=%async_computation.1 | async-start | bytes 1179648 | tf_op jit(solution)/shard_map/all_to_all | solution.py:646
  159.0 13.5 %copy-start.5 = (f32[59]{0:T(128)S(1)}, f32[59]{0:T(128)}, u32[]{:S(2)}) copy-start(f32[59]{0:T(128)} %constant.8.clone) | copy-start | bytes 712
  172.6 0.8 copy-start.1

commit v2 on v1

--- a/solution.py
+++ b/solution.py
@@ -180,7 +180,7 @@
         for f in range(FEATS):
             table_ref[pl.ds((camera * FEATS + f) * BLOCKS, BLOCKS), :] = features[f]
 
-    @pl.loop(0, VIEWS)
+    @pl.loop(0, VIEWS, unroll=2)
     def _(camera):
         chosen = index_ref[pl.ds(pl.multiple_of(camera * 8, 8), 8), :]
         low = jnp.bitwise_and(chosen, LANES - 1)
@@ -222,30 +222,27 @@
             preferred_element_type=jnp.float32,
         )
 
-    total = lax.fori_loop(0, LANES // 2, step, jnp.zeros((LANES, 2 * LANES), jnp.float32), unroll=4)
+    total = lax.fori_loop(0, LANES // 2, step, jnp.zeros((LANES, 2 * LANES), jnp.float32), unroll=8)
     lane_ref[...] = total[:, :LANES].astype(jnp.int32)
     row_ref[...] = total[:, LANES:].astype(jnp.int32) - 1
 
 
-def lane_gather(table, stride_row, stride_feature, low, high, store):
-    spans = len(low)
-
-    def step(source, totals):
-        totals = list(totals)
-        here = [h == source for h in high]
-        for f in range(FEATS):
-            line = table[pl.ds(source * stride_row + f * stride_feature, 1), :]
-            line = jnp.broadcast_to(line, (8, LANES))
-            for u in range(spans):
-                picked = jnp.take_along_axis(line, low[u], axis=1)
-                totals[f * spans + u] = jnp.where(here[u], picked, totals[f * spans + u])
-        return tuple(totals)
-
-    blank = tuple(jnp.zeros((8, LANES), jnp.float32) for _ in range(FEATS * spans))
-    totals = lax.fori_loop(0, LANES, step, blank, unroll=16)
-    for f in range(FEATS):
-        for u in range(spans):
-            store(f, u, totals[f * spans + u])
+def picked_lanes(table, first, low, high, base, count, totals):
+    for step in range(count):
+        source = base + step
+        here = high == source
+        for number, place in enumerate(first):
+            line = jnp.broadcast_to(table[pl.ds(place(source), 1), :], (8, LANES))
+            picked = jnp.take_along_axis(line, low, axis=1)
+            totals[number] = jnp.where(here, picked, totals[number])
+    return totals
+
+
+LANE_IN = (0, 1, 5)
+DOT_IN = (2, 3, 4, 6, 7, 8)
+LANE_OUT = (0, 1, 5)
+DOT_OUT = (2, 3, 4, 6, 7, 8)
+CONTRACT = (((1,), (1,)), ((), ()))
 
 
 KROWS = 32
@@ -271,6 +268,8 @@
     push_ref,
     grad_ref,
     moment_ref,
+    halves_ref,
+    sums_ref,
 ):
     render = lax.axis_index(AXES[1])
     device = lax.axis_index(AXES[0]) * lax.axis_size(AXES[1]) + render
@@ -278,18 +277,49 @@
     lane_tile = jnp.bitwise_and(lax.broadcasted_iota(jnp.int32, (8, LANES), 1), 7)
     centre_x = 16.0 * lane_tile.astype(jnp.float32) + 8.0
 
-    @pl.loop(0, 8)
-    def _(part):
-        spans = [pl.ds(pl.multiple_of(part * 16 + u * 8, 8), 8) for u in range(2)]
-        entries = [list_ref[span, :] for span in spans]
-        low = [jnp.bitwise_and(entry, CAP - 1) for entry in entries]
-        high = [jnp.right_shift(entry, 7) for entry in entries]
-
-        def store(f, u, value):
-            feat_ref[pl.ds(pl.multiple_of(f * LANES + part * 16 + u * 8, 8), 8), :] = value
-
-        lane_gather(table_ref, FEATS, 1, low, high, store)
-
+    owner = lax.broadcasted_iota(jnp.int32, (LANES, 2 * LANES), 0)
+    for number, f in enumerate(DOT_IN):
+        value = table_ref[pl.ds(f, DEVICES, stride=FEATS), :]
+        for which, part in enumerate(parts_of(value, 3)):
+            halves_ref[pl.ds(number * LANES, LANES), pl.ds(which * LANES, LANES)] = part
+
+    def collect(count, totals):
+        octet = count // 4
+        quarter = lax.rem(count, 4)
+        span = pl.ds(pl.multiple_of(octet * 8, 8), 8)
+        low = jnp.bitwise_and(list_ref[span, :], CAP - 1)
+        high = jnp.right_shift(list_ref[span, :], 7)
+        totals = [jnp.where(quarter == 0, 0.0, total) for total in totals]
+        first = [lambda source, f=f: source * FEATS + f for f in LANE_IN]
+        totals = picked_lanes(table_ref, first, low, high, quarter * 32, 32, totals)
+        for number, f in enumerate(LANE_IN):
+            feat_ref[pl.ds(pl.multiple_of(f * LANES + octet * 8, 8), 8), :] = totals[number]
+        lines = [list_ref[pl.ds(count * 2 + member, 1), :] for member in range(2)]
+        line = jnp.broadcast_to(jnp.concatenate(lines, 1), (LANES, 2 * LANES))
+        slot = jnp.where(jnp.bitwise_and(line, CAP - 1) == owner, 1.0, 0.0).astype(jnp.bfloat16)
+        thrice = jnp.concatenate([slot, slot, slot], 0)
+        exact = jnp.dot(
+            halves_ref[pl.ds(0, 3 * LANES), :], thrice, preferred_element_type=jnp.float32
+        )
+        other = jnp.dot(
+            halves_ref[pl.ds(3 * LANES, 3 * LANES), pl.ds(0, 2 * LANES)],
+            thrice[: 2 * LANES],
+            preferred_element_type=jnp.float32,
+        )
+        found = [exact[k * LANES : (k + 1) * LANES] for k in range(3)]
+        found += [other[k * LANES : (k + 1) * LANES] for k in range(3)]
+        mine = jnp.right_shift(line, 7) == owner
+        for number, f in enumerate(DOT_IN):
+            value = jnp.where(mine, found[number], 0.0)
+            value = jnp.sum(value, 0, keepdims=True)
+            for member in range(2):
+                feat_ref[pl.ds(f * LANES + count * 2 + member, 1), :] = value[
+                    :, member * LANES : (member + 1) * LANES
+                ]
+        return tuple(totals)
+
+    blank = tuple(jnp.zeros((8, LANES), jnp.float32) for _ in LANE_IN)
+    lax.fori_loop(0, LANES // 2, collect, blank, unroll=8)
     zero = jnp.zeros((8, LANES), jnp.float32)
 
     @pl.loop(0, 16)
@@ -320,30 +350,45 @@
 
     @pl.loop(0, SLABS)
     def _(group):
-        @pl.loop(0, 32, unroll=2)
-        def _(line):
-            start = pl.multiple_of((group * 32 + line) * KROWS, KROWS)
-            left = coef_ref[pl.ds(start, KROWS), :].T.astype(jnp.bfloat16)
-            wide = jnp.dot(left, expand_ref[...], preferred_element_type=jnp.float32)
-            out = pl.ds(pl.multiple_of(line * LANES, LANES), LANES)
+        @pl.loop(0, 8, unroll=4)
+        def _(quad):
+            lefts = []
+            for sub in range(4):
+                start = pl.multiple_of((group * 32 + quad * 4 + sub) * KROWS, KROWS)
+                lefts.append(coef_ref[pl.ds(start, KROWS), :].T.astype(jnp.bfloat16))
+            wide = jnp.dot(jnp.concatenate(lefts, 0), expand_ref[...], preferred_element_type=jnp.float32)
+            out = pl.ds(pl.multiple_of(quad * 512, 512), 512)
             alpha_ref[out, :] = wide[:, :PIX]
             colour_ref[out, :] = wide[:, PIX:]
 
         def forward(block, carry):
             through = list(carry[:2])
             image = list(carry[2:])
-            for u in range(16):
-                here = pl.ds(pl.multiple_of(block * LANES + u * 8, 8), 8)
-                shade = [colour_ref[here, pl.ds(k * LANES, LANES)] for k in range(3)]
-                for half in range(2):
-                    cols = pl.ds(half * LANES, LANES)
-                    alpha = jnp.minimum(jnp.exp2(alpha_ref[here, cols]), 0.99)
-                    weight = alpha * through[half]
-                    through[half] = through[half] * (1.0 - alpha)
-                    alpha_ref[here, cols] = alpha
-                    weight_ref[here, cols] = weight
-                    for k in range(3):
-                        image[k * 2 + half] = image[k * 2 + half] + shade[k] * weight
+            for lot in range(2):
+                alphas, weights, spots = [], [], []
+                for u in range(8):
+                    here = pl.ds(pl.multiple_of(block * LANES + (lot * 8 + u) * 8, 8), 8)
+                    spots.append(here)
+                    alphas.append(
+                        [
+                            jnp.minimum(jnp.exp2(alpha_ref[here, pl.ds(half * LANES, LANES)]), 0.99)
+                            for half in range(2)
+                        ]
+                    )
+                for u in range(8):
+                    shade = [colour_ref[spots[u], pl.ds(k * LANES, LANES)] for k in range(3)]
+                    weights.append([])
+                    for half in range(2):
+                        weight = alphas[u][half] * through[half]
+                        through[half] = through[half] * (1.0 - alphas[u][half])
+                        weights[u].append(weight)
+                        for k in range(3):
+                            image[k * 2 + half] = image[k * 2 + half] + shade[k] * weight
+                for u in range(8):
+                    for half in range(2):
+                        cols = pl.ds(half * LANES, LANES)
+                        alpha_ref[spots[u], cols] = alphas[u][half]
+                        weight_ref[spots[u], cols] = weights[u][half]
             return tuple(through + image)
 
         ones = jnp.ones((8, LANES), jnp.float32)
@@ -361,6 +406,7 @@
             block = 31 - count
             for pair in range(7, -1, -1):
                 pushes = [[None, None], [None, None]]
+                loads = [[None, None], [None, None]]
                 for member in (1, 0):
                     here = pl.ds(pl.multiple_of(block * LANES + pair * 16 + member * 8, 8), 8)
                     shade = [colour_ref[here, pl.ds(k * LANES, LANES)] for k in range(3)]
@@ -373,14 +419,16 @@
                             + shade[1] * residual[2 + half]
                             + shade[2] * residual[4 + half]
                         )
+                        loads[half][member] = weight
                         gain = worth - behind[half]
                         behind[half] = behind[half] + alpha * gain
                         pushes[half][member] = jnp.where(alpha < 0.99, weight * gain, 0.0)
                 rows = pl.ds(pl.multiple_of(block * LANES + pair * 16, 16), 16)
                 for half in range(2):
-                    value = jnp.concatenate(pushes[half], 0)
-                    for which, part in enumerate(parts_of(value, 2)):
-                        push_ref[which, rows, pl.ds(half * LANES, LANES)] = part
+                    parts = parts_of(jnp.concatenate(pushes[half], 0), 2)
+                    parts += parts_of(jnp.concatenate(loads[half], 0), 2)
+                    for which, part in enumerate(parts):
+                        push_ref[rows, pl.ds(which * PIX + half * LANES, LANES)] = part
             return tuple(behind)
 
         lax.fori_loop(0, 32, backward, (zero, zero))
@@ -388,23 +436,22 @@
             [jnp.concatenate([residual[k * 2], residual[k * 2 + 1]], 1) for k in range(3)], 0
         )
         stack = jnp.concatenate(parts_of(stack, 2), 0)
-        contract = (((1,), (1,)), ((), ()))
-
-        @pl.loop(0, 8)
+        stack = jnp.concatenate([stack, stack], 1)
+        powers = jnp.concatenate([mono_ref[...], mono_ref[...]], 1)
+
+        @pl.loop(0, 2)
         def _(chunk):
-            rows = pl.ds(pl.multiple_of(chunk * 512, 512), 512)
+            rows = pl.ds(pl.multiple_of(chunk * 2048, 2048), 2048)
             moments = lax.dot_general(
-                mono_ref[...], push_ref[0, rows, :], contract, preferred_element_type=jnp.float32
-            ) + lax.dot_general(
-                mono_ref[...], push_ref[1, rows, :], contract, preferred_element_type=jnp.float32
+                powers, push_ref[rows, pl.ds(0, 2 * PIX)], CONTRACT, preferred_element_type=jnp.float32
             )
-            tints = 0.0
-            for part in parts_of(weight_ref[rows, :], 2):
-                tints = tints + lax.dot_general(stack, part, contract, preferred_element_type=jnp.float32)
+            tints = lax.dot_general(
+                stack, push_ref[rows, pl.ds(2 * PIX, 2 * PIX)], CONTRACT, preferred_element_type=jnp.float32
+            )
             tints = tints[:24] + tints[24:]
-            for line in range(4):
+            for line in range(16):
                 cols = slice(line * LANES, (line + 1) * LANES)
-                base = ((group * 32) + chunk * 4 + line) * GRADS
+                base = ((group * 32) + chunk * 16 + line) * GRADS
                 moment_ref[pl.ds(pl.multiple_of(base, 8), 8), :] = moments[:8, cols]
                 for k in range(3):
                     own = jnp.where(diagonal, tints[k * 8 : k * 8 + 8, cols], 0.0)
@@ -437,16 +484,62 @@
         for f in range(FEATS):
             grad_ref[pl.ds(pl.multiple_of(f * LANES + octet * 8, 8), 8), :] = results[f]
 
-    @pl.loop(0, 8)
-    def _(part):
-        spans = [pl.ds(pl.multiple_of(part * 16 + u * 8, 8), 8) for u in range(2)]
-        low = [lane_ref[span, :] for span in spans]
-        high = [row_ref[span, :] for span in spans]
-
-        def store(f, u, value):
-            back_ref[pl.ds((part * 16 + u * 8) * FEATS + f, 8, stride=FEATS), :] = value
-
-        lane_gather(grad_ref, 1, LANES, low, high, store)
+    sums_ref[...] = jnp.zeros(sums_ref.shape, jnp.float32)
+    half_owner = lax.broadcasted_iota(jnp.int32, (LANES // 2, LANES), 0)
+    place = lax.broadcasted_iota(jnp.int32, (2 * LANES, LANES), 0)
+
+    def spread_out(count, totals):
+        octet = count // 4
+        quarter = lax.rem(count, 4)
+        span = pl.ds(pl.multiple_of(octet * 8, 8), 8)
+        totals = [jnp.where(quarter == 0, 0.0, total) for total in totals]
+        first = [lambda source, f=f: f * LANES + source for f in LANE_OUT]
+        totals = picked_lanes(
+            grad_ref, first, lane_ref[span, :], row_ref[span, :], quarter * 32, 32, totals
+        )
+        for number, f in enumerate(LANE_OUT):
+            back_ref[pl.ds(octet * 8 * FEATS + f, 8, stride=FEATS), :] = totals[number]
+        slots = []
+        owners = []
+        for member in range(2):
+            line = list_ref[pl.ds(count * 2 + member, 1), :]
+            half = jnp.bitwise_and(jnp.right_shift(line, 7), LANES // 2 - 1)
+            half = jnp.where(line < 0, -1, half)
+            spot = jnp.right_shift(line, 13) * LANES + jnp.bitwise_and(line, CAP - 1)
+            owners.append(jnp.broadcast_to(half, (LANES // 2, LANES)) == half_owner)
+            same = jnp.broadcast_to(spot, (2 * LANES, LANES)) == place
+            slots.append(jnp.where(same, 1.0, 0.0).astype(jnp.bfloat16))
+        rows = []
+        for f in DOT_OUT:
+            lines = [grad_ref[pl.ds(f * LANES + count * 2 + member, 1), :] for member in range(2)]
+            tops = [line.astype(jnp.bfloat16).astype(jnp.float32) for line in lines]
+            pieces = tops + [line - top for line, top in zip(lines, tops)]
+            rows.append(
+                jnp.concatenate(
+                    [
+                        jnp.where(
+                            owners[number % 2], jnp.broadcast_to(piece, (LANES // 2, LANES)), 0.0
+                        ).astype(jnp.bfloat16)
+                        for number, piece in enumerate(pieces)
+                    ],
+                    1,
+                )
+            )
+        sums_ref[...] += lax.dot_general(
+            jnp.concatenate(rows, 0),
+            jnp.concatenate(slots + slots, 1),
+            CONTRACT,
+            preferred_element_type=jnp.float32,
+        )
+        return tuple(totals)
+
+    blank = tuple(jnp.zeros((8, LANES), jnp.float32) for _ in LANE_OUT)
+    lax.fori_loop(0, LANES // 2, spread_out, blank, unroll=8)
+    for number, f in enumerate(DOT_OUT):
+        for side in range(2):
+            back_ref[pl.ds(side * (LANES // 2) * FEATS + f, LANES // 2, stride=FEATS), :] = sums_ref[
+                pl.ds(number * (LANES // 2), LANES // 2), pl.ds(side * LANES, LANES)
+            ]
 
 
 SUM_PARTS = 2
@@ -462,7 +555,7 @@
     sublane = lax.broadcasted_iota(jnp.int32, (LANES, LANES), 0)
     short = lax.broadcasted_iota(jnp.int32, (BLOCKS, LANES), 0)
 
-    @pl.loop(0, VIEWS)
+    @pl.loop(0, VIEWS, unroll=2)
     def _(camera):
         total = jnp.zeros((SUM_PARTS * FEATS * BLOCKS, LANES), jnp.float32)
         for pair in range(4):
@@ -607,9 +700,11 @@
             buffer(GROUP_ROWS, PIX),
             buffer(GROUP_ROWS, PIX),
             buffer(GROUP_ROWS, 3 * LANES),
-            buffer(2, GROUP_ROWS, PIX, dtype=jnp.bfloat16),
+            buffer(GROUP_ROWS, 4 * PIX, dtype=jnp.bfloat16),
             buffer(FEATS * LANES, LANES),
             buffer(LANES * GRADS, LANES),
+            buffer(len(DOT_IN) * LANES, 3 * LANES, dtype=jnp.bfloat16),
+            buffer(len(DOT_OUT) * LANES // 2, 2 * LANES),
         ],
         received,
         entries,

time: 187 us -> 133 us (0.71)
  Pallas kernels: 146 us -> 91.3 us
    pallas_call x4, Pallas kernels: 146 us -> 91.3 us  [run_kernel(): pl.pallas_call(kernel, out_shape=shapes, in_specs=[WHOLE] * len(operands)...]
  transfers between devices with their start and end apart: 2 -> 2, of which waited for: 2 -> 2; matrix products, arithmetic and copies ran while one was open for 1% -> 2% of each run, Pallas kernels for 4% -> 4%
where the time goes in v2:
time: 133 us
  Pallas kernels  91.3 us (69%)
  waiting for transfers between devices  19.7 us (15%)
  starting transfers between devices  16.3 us (12%)
  local copies, waits for them, and re-layouts  4.56 us (3%)
    pallas_call x4, Pallas kernels, run_kernel(): pl.pallas_call(kernel, out_shape=shapes, in_specs=[WHOLE] * len(operands)...  91.3 us
    all_to_all x2, waiting for transfers between devices, exchange(): lax.all_to_all(chunks, AXES, split_axis=0, concat_axis=0, tiled=True)  19.7 us
    all_to_all x2, starting transfers between devices, exchange(): lax.all_to_all(chunks, AXES, split_axis=0, concat_axis=0, tiled=True)  16.3 us
  transfers between devices with their start and end apart: 2, of which 2 were waited for; matrix products, arithmetic and copies ran while one was open for 2% of the time, Pallas kernels for 4%

profile of v2, /device:TPU:1, one launch (start us, length us, event | category | flops | bytes accessed | tf_op | source)
XLA Modules:
  0.0 132.6 jit_solution(3004631722655969689)
XLA Ops:
  0.6 8.9 %shard_map.120 = f32[1152,128]{1,0:T(8,128)} custom-call(f32[59,2048]{1,0:T(8,128)} %params_ref.3, s32[128,128]{1,0:T(8,128)} %bitcast.19), custom_call_target="tpu_custom_call" | custom-call | tf_op jit(solution)/shard_map/pallas_call | solution.py:642
  9.6 0.0 copy-start.2
  9.6 11.5 %all-to-all-start = ((f32[128,1,1152]{2,1,0:T(1,128)}), f32[128,1,1152]{2,1,0:T(1,128)S(1)}, u32[]{:S(2)}, u32[]{:S(2)}) async-start(f32[128,1,1152]{2,1,0:T(1,128)} %bitcast.15), calls=%async_computation | async-start | bytes 1179648 | tf_op jit(solution)/shard_map/all_to_all | solution.py:741
  21.1 0.0 copy-done.2
  21.1 0.0 copy-start.4
  21.1 0.6 copy.25
  21.8 0.2 copy-done.4
  21.9 0.3 copy.20
  22.3 1.1 reshape.35.list_ref
  23.4 5.6 %shard_map.121 = (s32[128,128]{1,0:T(8,128)}, s32[128,128]{1,0:T(8,128)}) custom-call(s32[128,128]{1,0:T(8,128)} %reshape.35.list_ref), custom_call_target="tpu_custom_call" | custom-call | tf_op jit(solution)/shard_map/pallas_call | solution.py:642
  28.9 6.2 %all-to-all-done = f32[128,1,1152]{2,1,0:T(1,128)S(1)} async-done(((f32[128,1,1152]{2,1,0:T(1,128)}), f32[128,1,1152]{2,1,0:T(1,128)S(1)}, u32[]{:S(2)}, u32[]{:S(2)}) %all-to-all-start) | async-done | bytes 589856 | tf_op jit(solution)/shard_map/all_to_all | solution.py:741
  35.1 0.0 copy-start
  35.1 0.8 copy-done
  36.0 65.0 %shard_map.122 = (f32[32,768]{1,0:T(8,128)}, f32[1152,128]{1,0:T(8,128)}) custom-call(f32[1152,128]{1,0:T(8,128)} %bitcast.14, s32[128,128]{1,0:T(8,128)} %reshape.35.list_ref, s32[128,128]{1,0:T(8,128)} %get-tuple-element.11.lane_ref, s32[128,128]{1,0:T(8,128)} %get-tuple-element.12.row_ref, f32[32,768]{1,0:T(8,128)} %bitcast.18, ...), custom_call_target="tpu_custom_call" | custom-call | tf_op jit(solution)/shard_map/pallas_call | solution.py:642
  101.0 0.0 copy-start.3
  101.0 4.8 %all-to-all-start.1 = ((f32[128,1,1152]{2,1,0:T(1,128)}), f32[128,1,1152]{2,1,0:T(1,128)S(1)}, u32[]{:S(2)}, u32[]{:S(2)}) async-start(f32[128,1,1152]{2,1,0:T(1,128)} %bitcast.17), calls=%async_computation.1 | async-start | bytes 1179648 | tf_op jit(solution)/shard_map/all_to_all | solution.py:741
  105.9 0.0 copy-done.3
  105.9 0.6 copy.27
  106.5 0.0 copy-start.5
  106.5 13.5 %all-to-all-done.1 = f32[128,1,1152]{2,1,0:T(1,128)S(1)} async-done(((f32[128,1,1152]{2,1,0:T(1,128)}), f32[128,1,1152]{2,1,0:T(1,128)S(1)}, u32[]{:S(2)}, u32[]{:S(2)}) %all-to-all-start.1) | async-done | bytes 589856 | tf_op jit(solution)/shard_map/all_to_all | solution.py:741
  120.1 0.0 copy-done.5
  120.1 0.8 jit_solution_.3.rate_ref
  120.9 0.0 copy-done.1
  120.9 11.7 %shard_map.123 = (f32[59,2048]{1,0:T(8,128)}, f32[59,2048]{1,0:T(8,128)}, f32[59,2048]{1,0:T(8,128)}) custom-call(f32[1152,128]{1,0:T(8,128)} %bitcast.16, s32[128,128]{1,0:T(8,128)} %bitcast.20, f32[59,2048]{1,0:T(8,128)} %params_ref.3, f32[59,2048]{1,0:T(8,128)} %first_ref.1, f32[59,2048]{1,0:T(8,128)} %second_ref.1, f32[59,128]{1,0:T(8,128)} %jit_solution_.3.rate_ref), custom_call_target="tpu_custom_call" | custom-call | tf_op jit(solution)/shard_map/pallas_call | solution.py:642
  (1 shorter events, 0.0 us)
Async XLA Ops:
  9.6 11.5 %copy-start.2 = (f32[32,3,256]{2,0,1:T(8,128)S(1)}, f32[32,3,256]{2,0,1:T(8,128)}, u32[]{:S(2)}) copy-start(f32[32,3,256]{2,0,1:T(8,128)} %param.12) | copy-start | bytes 294916
  9.6 25.6 %all-to-all-start = ((f32[128,1,1152]{2,1,0:T(1,128)}), f32[128,1,1152]{2,1,0:T(1,128)S(1)}, u32[]{:S(2)}, u32[]{:S(2)}) async-start(f32[128,1,1152]{2,1,0:T(1,128)} %bitcast.15), calls=%async_computation | async-start | bytes 1179648 | tf_op jit(solution)/shard_map/all_to_all | solution.py:741
  21.1 0.8 copy-start.4
  35.1 0.8 copy-start
  101.0 4.9 %copy-start.3 = (f32[32,768]{1,0:T(8,128)S(1)}, f32[32,768]{1,0:T(8,128)}, u32[]{:S(2)}) copy-start(f32[32,768]{1,0:T(8,128)} %get-tuple-element.13) | copy-start | bytes 294916
  101.0 19.0 %all-to-all-start.1 = ((f32[128,1,1152]{2,1,0:T(1,128)}), f32[128,1,1152]{2,1,0:T(1,128)S(1)}, u32[]{:S(2)}, u32[]{:S(2)}) async-start(f32[128,1,1152]{2,1,0:T(1,128)} %bitcast.17), calls=%async_computation.1 | async-start | bytes 1179648 | tf_op jit(solution)/shard_map/all_to_all | solution.py:741
  106.5 13.5 %copy-start.5 = (f32[59]{0:T(128)S(1)}, f32[59]{0:T(128)}, u32[]{:S(2)}) copy-start(f32[59]{0:T(128)} %constant.8.clone) | copy-start | bytes 712
  120.1 0.8 copy-start.1

commit v3 on v2

--- a/solution.py
+++ b/solution.py
@@ -24,6 +24,7 @@
 SLABS = 4
 LOG2E = 1.4426950408889634
 AXES = ("gauss", "render")
+CONTRACT = (((1,), (1,)), ((), ()))
 VMEM_LIMIT = 56 * 1024 * 1024
 
 sh_first = 0.28209479177387814
@@ -164,40 +165,64 @@
     return parts
 
 
-def project_kernel(params_ref, index_ref, out_ref, rows_ref, table_ref):
-    block_rows(params_ref, rows_ref)
-    row = functools.partial(strided, rows_ref)
-    sigma = spread([row(3 + k) for k in range(3)], [row(6 + k) for k in range(4)])
-    logit = row(10)
-    log_opacity = -LOG2E * (jnp.maximum(-logit, 0.0) + jnp.log1p(jnp.exp(-jnp.abs(logit))))
-    for camera in range(VIEWS):
-        lean_x, lean_y, shift_x, shift_y, basis = CAMERAS[camera]
-        height = row(2)
-        features = [row(0) + lean_x * height - shift_x, row(1) + lean_y * height - shift_y]
-        features += list(conic_of(sigma, lean_x, lean_y))
-        features.append(log_opacity)
-        features += [jnp.maximum(raw_colour(row, basis, k), 0.0) for k in range(3)]
-        for f in range(FEATS):
-            table_ref[pl.ds((camera * FEATS + f) * BLOCKS, BLOCKS), :] = features[f]
-
-    @pl.loop(0, VIEWS, unroll=2)
-    def _(camera):
-        chosen = index_ref[pl.ds(pl.multiple_of(camera * 8, 8), 8), :]
-        low = jnp.bitwise_and(chosen, LANES - 1)
-        high = jnp.right_shift(chosen, 7)
-        totals = [jnp.zeros((8, LANES), jnp.float32) for _ in range(FEATS)]
-        for block in range(BLOCKS):
-            here = high == block
-            for f in range(FEATS):
-                line = table_ref[pl.ds((camera * FEATS + f) * BLOCKS + block, 1), :]
-                line = jnp.broadcast_to(line, (8, LANES))
-                picked = jnp.take_along_axis(line, low, axis=1)
-                totals[f] = jnp.where(here, picked, totals[f])
-        for f in range(FEATS):
-            out_ref[pl.ds(camera * 8 * FEATS + f, 8, stride=FEATS), :] = totals[f]
-
-
-def invert_kernel(list_ref, lane_ref, row_ref):
+MESH = pl.DeviceIdType.MESH
+
+
+def own_number():
+    return lax.axis_index(AXES[0]) * lax.axis_size(AXES[1]) + lax.axis_index(AXES[1])
+
+
+def coordinates(number):
+    across = lax.axis_size(AXES[1])
+    return (number // across, lax.rem(number, across))
+
+
+def announce():
+    me = own_number()
+    barrier = pltpu.get_barrier_semaphore()
+
+    def tell(step, carry):
+        pl.semaphore_signal(
+            barrier,
+            inc=1,
+            device_id=coordinates(lax.rem(me + step, DEVICES)),
+            device_id_type=MESH,
+        )
+        return carry
+
+    lax.fori_loop(1, DEVICES, tell, 0, unroll=True)
+    return barrier
+
+
+def send_chunk(target, me, send_ref, recv_ref, send_sem, recv_sem):
+    pltpu.make_async_remote_copy(
+        src_ref=send_ref.at[target],
+        dst_ref=recv_ref.at[me],
+        send_sem=send_sem,
+        recv_sem=recv_sem,
+        device_id=coordinates(target),
+        device_id_type=MESH,
+    ).start()
+
+
+def all_chunks(me, send_ref, recv_ref, send_sem, recv_sem):
+    most = pl.ds(0, DEVICES - 1)
+    return pltpu.make_async_remote_copy(
+        src_ref=send_ref.at[most],
+        dst_ref=recv_ref.at[most],
+        send_sem=send_sem,
+        recv_sem=recv_sem,
+        device_id=coordinates(me),
+        device_id_type=MESH,
+    )
+
+
+def flatten_chunks(recv_ref, out_ref):
+    for source in range(DEVICES):
+        out_ref[pl.ds(source * FEATS, FEATS), :] = recv_ref[source]
+
+
+def invert_lists(list_ref, lane_ref, row_ref):
     sublane = lax.broadcasted_iota(jnp.int32, (LANES, LANES), 0)
     lane = lax.broadcasted_iota(jnp.int32, (LANES, LANES), 1).astype(jnp.float32)
 
@@ -218,13 +243,88 @@
         return total + lax.dot_general(
             jnp.concatenate(owners, 1),
             jnp.concatenate(slots, 1),
-            (((1,), (1,)), ((), ())),
+            CONTRACT,
             preferred_element_type=jnp.float32,
         )
 
     total = lax.fori_loop(0, LANES // 2, step, jnp.zeros((LANES, 2 * LANES), jnp.float32), unroll=8)
     lane_ref[...] = total[:, :LANES].astype(jnp.int32)
     row_ref[...] = total[:, LANES:].astype(jnp.int32) - 1
+
+
+def deliver_kernel(
+    params_ref, index_ref, list_ref,
+    out_ref, lane_ref, row_ref,
+    rows_ref, table_ref, flat_ref, send_ref, recv_ref, send_sem, recv_sem,
+):
+    me = own_number()
+    barrier = announce()
+    block_rows(params_ref, rows_ref)
+    row = functools.partial(strided, rows_ref)
+    sigma = spread([row(3 + k) for k in range(3)], [row(6 + k) for k in range(4)])
+    logit = row(10)
+    log_opacity = -LOG2E * (jnp.maximum(-logit, 0.0) + jnp.log1p(jnp.exp(-jnp.abs(logit))))
+    for camera in range(VIEWS):
+        lean_x, lean_y, shift_x, shift_y, basis = CAMERAS[camera]
+        height = row(2)
+        features = [row(0) + lean_x * height - shift_x, row(1) + lean_y * height - shift_y]
+        features += list(conic_of(sigma, lean_x, lean_y))
+        features.append(log_opacity)
+        features += [jnp.maximum(raw_colour(row, basis, k), 0.0) for k in range(3)]
+        for f in range(FEATS):
+            table_ref[pl.ds((camera * FEATS + f) * BLOCKS, BLOCKS), :] = features[f]
+    pl.semaphore_wait(barrier, DEVICES - 1)
+
+    @pl.loop(0, VIEWS)
+    def _(turn):
+        camera = lax.rem(me // (DEVICES // VIEWS) + turn, VIEWS)
+        chosen = index_ref[pl.ds(pl.multiple_of(camera * 8, 8), 8), :]
+        low = jnp.bitwise_and(chosen, LANES - 1)
+        high = jnp.right_shift(chosen, 7)
+        totals = [jnp.zeros((8, LANES), jnp.float32) for _ in range(FEATS)]
+        for block in range(BLOCKS):
+            here = high == block
+            for f in range(FEATS):
+                line = table_ref[pl.ds((camera * FEATS + f) * BLOCKS + block, 1), :]
+                line = jnp.broadcast_to(line, (8, LANES))
+                picked = jnp.take_along_axis(line, low, axis=1)
+                totals[f] = jnp.where(here, picked, totals[f])
+        for f in range(FEATS):
+            flat_ref[pl.ds(f, 8, stride=FEATS), :] = totals[f]
+        for member in range(8):
+            send_ref[camera * 8 + member] = flat_ref[pl.ds(member * FEATS, FEATS), :]
+        for step in range(8):
+            target = camera * 8 + lax.rem(me + step, 8)
+
+            @pl.when(target != me)
+            def _():
+                send_chunk(target, me, send_ref, recv_ref, send_sem, recv_sem)
+
+    invert_lists(list_ref, lane_ref, row_ref)
+    whole = all_chunks(me, send_ref, recv_ref, send_sem, recv_sem)
+    recv_ref[me] = send_ref[me]
+    whole.wait_recv()
+    flatten_chunks(recv_ref, out_ref)
+    whole.wait_send()
+
+
+def return_kernel(back_ref, out_ref, send_ref, recv_ref, send_sem, recv_sem):
+    me = own_number()
+    barrier = announce()
+    for target in range(DEVICES):
+        send_ref[target] = back_ref[pl.ds(target * FEATS, FEATS), :]
+    pl.semaphore_wait(barrier, DEVICES - 1)
+
+    def send(step, carry):
+        send_chunk(lax.rem(me + step, DEVICES), me, send_ref, recv_ref, send_sem, recv_sem)
+        return carry
+
+    lax.fori_loop(1, DEVICES, send, 0, unroll=8)
+    whole = all_chunks(me, send_ref, recv_ref, send_sem, recv_sem)
+    recv_ref[me] = send_ref[me]
+    whole.wait_recv()
+    flatten_chunks(recv_ref, out_ref)
+    whole.wait_send()
 
 
 def picked_lanes(table, first, low, high, base, count, totals):
@@ -242,9 +342,6 @@
 DOT_IN = (2, 3, 4, 6, 7, 8)
 LANE_OUT = (0, 1, 5)
 DOT_OUT = (2, 3, 4, 6, 7, 8)
-CONTRACT = (((1,), (1,)), ((), ()))
-
-
 KROWS = 32
 GRADS = 16
 GROUP_ROWS = LIST * 8
@@ -637,15 +734,18 @@
 WHOLE = pl.BlockSpec(memory_space=pltpu.VMEM)
 
 
-def run_kernel(kernel, shapes, scratch, *operands):
+def run_kernel(kernel, shapes, scratch, *operands, collective_id=None):
     many = isinstance(shapes, list)
+    extra = {}
+    if collective_id is not None:
+        extra = dict(collective_id=collective_id, has_side_effects=True)
     return pl.pallas_call(
         kernel,
         out_shape=shapes,
         in_specs=[WHOLE] * len(operands),
         out_specs=[WHOLE] * len(shapes) if many else WHOLE,
         scratch_shapes=scratch,
-        compiler_params=pltpu.CompilerParams(vmem_limit_bytes=VMEM_LIMIT),
+        compiler_params=pltpu.CompilerParams(vmem_limit_bytes=VMEM_LIMIT, **extra),
     )(*operands)
 
 
@@ -671,22 +771,36 @@
     return jnp.asarray(wide, jnp.bfloat16), jnp.asarray(narrow, jnp.bfloat16)
 
 
-def owner_features(params, index):
+def chunk_buffers():
+    chunks = buffer(DEVICES, FEATS, LANES)
+    return [chunks, chunks, pltpu.SemaphoreType.DMA, pltpu.SemaphoreType.DMA]
+
+
+def deliver(params, index, entries):
     return run_kernel(
-        project_kernel,
-        table(DEVICES * FEATS),
-        [buffer(BLOCKS * PROWS, LANES), buffer(VIEWS * FEATS * BLOCKS, LANES)],
+        deliver_kernel,
+        [table(DEVICES * FEATS)] + [table(LANES, jnp.int32)] * 2,
+        [
+            buffer(BLOCKS * PROWS, LANES),
+            buffer(VIEWS * FEATS * BLOCKS, LANES),
+            buffer(8 * FEATS, LANES),
+        ]
+        + chunk_buffers(),
         params,
         index,
+        entries,
+        collective_id=0,
+    )
+
+
+def give_back(returning):
+    return run_kernel(
+        return_kernel, table(DEVICES * FEATS), chunk_buffers(), returning, collective_id=1
     )
 
 
 def ordered(tile_lists):
     return tile_lists.reshape(SLABS, 8, LIST).transpose(0, 2, 1).reshape(LANES, LANES)
-
-
-def inverse_lists(entries):
-    return run_kernel(invert_kernel, [table(LANES, jnp.int32)] * 2, [], entries)
 
 
 def render(received, entries, lanes, rows, target):
@@ -736,21 +850,13 @@
     )
 
 
-def exchange(values):
-    chunks = values.reshape(DEVICES, 1, FEATS * LANES)
-    arrived = lax.all_to_all(chunks, AXES, split_axis=0, concat_axis=0, tiled=True)
-    return arrived.reshape(DEVICES * FEATS, LANES)
-
-
 def per_device(params, first_moment, second_moment, target_images, tile_lists, send_index):
     index = send_index[0]
-    outgoing = owner_features(params, index)
     entries = ordered(tile_lists)
-    received = exchange(outgoing)
-    lanes, rows = inverse_lists(entries)
+    received, lanes, rows = deliver(params, index, entries)
     target = target_images.reshape(TILE_DEV, 3 * PIX)
     image, returning = render(received, entries, lanes, rows, target)
-    back = exchange(returning)
+    back = give_back(returning)
     new_params, new_first, new_second = owner_update(back, index, params, first_moment, second_moment)
     return (image.reshape(target_images.shape), new_params, new_first, new_second)
 

time: 133 us -> 126 us (0.947)
  Pallas kernels: 91.3 us -> 120 us
  waiting for transfers between devices: 19.7 us -> 0 us
  starting transfers between devices: 16.3 us -> 0 us
    pallas_call x4, Pallas kernels: 91.3 us -> 120 us  [run_kernel(): pl.pallas_call(kernel, out_shape=shapes, in_specs=[WHOLE] * len(operands)...]
    all_to_all x2 -> x0, waiting for transfers between devices: 19.7 us -> none  [exchange(): lax.all_to_all(chunks, AXES, split_axis=0, concat_axis=0, tiled=True)]
    all_to_all x2 -> x0, starting transfers between devices: 16.3 us -> none  [exchange(): lax.all_to_all(chunks, AXES, split_axis=0, concat_axis=0, tiled=True)]
  transfers between devices with their start and end apart: 2 -> 0, of which waited for: 2 -> 0; matrix products, arithmetic and copies ran while one was open for 2% -> 0% of each run, Pallas kernels for 4% -> 0%
where the time goes in v3:
time: 126 us
  Pallas kernels  120 us (95%)
  local copies, waits for them, and re-layouts  5.21 us (4%)
    pallas_call x4, Pallas kernels, run_kernel(): pl.pallas_call(kernel, out_shape=shapes, in_specs=[WHOLE] * len(operands)...  120 us

profile of v3, /device:TPU:1, one launch (start us, length us, event | category | flops | bytes accessed | tf_op | source)
XLA Modules:
  0.0 125.9 jit_solution(13021338273183545203)
XLA Ops:
  0.6 0.0 copy-start
  0.6 1.6 %copy.20 = f32[3,4,8,256]{3,2,0,1:T(8,128)} copy(f32[3,4,8,256]{3,2,1,0:T(8,128)} %bitcast.13) | data formatting | bytes 196608 | tf_op jit(solution)/shard_map/reshape | solution.py:857
  2.2 0.0 copy-done
  2.2 0.3 copy.16
  2.5 1.1 reshape.21.list_ref
  3.6 24.3 %shard_map.120 = (f32[1152,128]{1,0:T(8,128)}, s32[128,128]{1,0:T(8,128)}, s32[128,128]{1,0:T(8,128)}) custom-call(f32[59,2048]{1,0:T(8,128)} %params_ref.3, s32[128,128]{1,0:T(8,128)} %bitcast.11, s32[128,128]{1,0:T(8,128)} %reshape.21.list_ref), custom_call_target="tpu_custom_call" | custom-call | tf_op jit(solution)/shard_map/pallas_call | solution.py:742
  28.0 65.1 %shard_map.121 = (f32[32,768]{1,0:T(8,128)}, f32[1152,128]{1,0:T(8,128)}) custom-call(f32[1152,128]{1,0:T(8,128)} %get-tuple-element.12.table_ref, s32[128,128]{1,0:T(8,128)} %reshape.21.list_ref, s32[128,128]{1,0:T(8,128)} %get-tuple-element.13.lane_ref, s32[128,128]{1,0:T(8,128)} %get-tuple-element.14.row_ref, f32[32,768]{1,0:T(8,128)} %bitcast.10, ...), custom_call_target="tpu_custom_call" | custom-call | tf_op jit(solution)/shard_map/pallas_call | solution.py:742
  93.0 1.5 %copy.22 = f32[4,3,8,256]{3,2,0,1:T(8,128)} copy(f32[4,3,8,256]{3,2,1,0:T(8,128)} %bitcast.15) | data formatting | bytes 196608 | tf_op jit(solution)/shard_map/reshape | solution.py:861
  94.6 0.0 copy-start.1
  94.6 18.7 %shard_map.122.back_ref = f32[1152,128]{1,0:T(8,128)} custom-call(f32[1152,128]{1,0:T(8,128)} %get-tuple-element.16.back_ref), custom_call_target="tpu_custom_call" | custom-call | tf_op jit(solution)/shard_map/pallas_call | solution.py:742
  113.3 0.0 copy-done.1
  113.3 0.7 jit_solution_.3.rate_ref
  113.9 11.9 %shard_map.123 = (f32[59,2048]{1,0:T(8,128)}, f32[59,2048]{1,0:T(8,128)}, f32[59,2048]{1,0:T(8,128)}) custom-call(f32[1152,128]{1,0:T(8,128)} %shard_map.122.back_ref, s32[128,128]{1,0:T(8,128)} %bitcast.12, f32[59,2048]{1,0:T(8,128)} %params_ref.3, f32[59,2048]{1,0:T(8,128)} %first_ref.1, f32[59,2048]{1,0:T(8,128)} %second_ref.1, ...), custom_call_target="tpu_custom_call" | custom-call | tf_op jit(solution)/shard_map/pallas_call | solution.py:742
Async XLA Ops:
  0.6 1.6 %copy-start = (s32[32,512]{1,0:T(8,128)S(1)}, s32[32,512]{1,0:T(8,128)}, u32[]{:S(2)}) copy-start(s32[32,512]{1,0:T(8,128)} %param.13) | copy-start | bytes 196612
  94.6 18.7 %copy-start.1 = (f32[59]{0:T(128)S(1)}, f32[59]{0:T(128)}, u32[]{:S(2)}) copy-start(f32[59]{0:T(128)} %constant.8.clone) | copy-start | bytes 712

commit v4 on v3

--- a/solution.py
+++ b/solution.py
@@ -53,15 +53,12 @@
 
 
 def rate_table():
-    table = np.full((PARAMS,), 0.000125)
-    table[0:3] = 0.0016
-    table[3:6] = 0.005
-    table[6:10] = 0.001
-    table[10] = 0.05
-    table[11] = 0.0025
-    table[27] = 0.0025
-    table[43] = 0.0025
-    return np.broadcast_to(table.astype(np.float32)[:, None], (PARAMS, LANES))
+    row = lax.broadcasted_iota(jnp.int32, (PARAMS, LANES), 0)
+    rates = jnp.where((row == 11) | (row == 27) | (row == 43), 0.0025, 0.000125)
+    rates = jnp.where(row == 10, 0.05, rates)
+    for last, rate in ((10, 0.001), (6, 0.005), (3, 0.0016)):
+        rates = jnp.where(row < last, rate, rates)
+    return rates.astype(jnp.float32)
 
 
 def sh_basis(dir_x, dir_y, dir_z):
@@ -252,7 +249,7 @@
     row_ref[...] = total[:, LANES:].astype(jnp.int32) - 1
 
 
-def deliver_kernel(
+def deliver(
     params_ref, index_ref, list_ref,
     out_ref, lane_ref, row_ref,
     rows_ref, table_ref, flat_ref, send_ref, recv_ref, send_sem, recv_sem,
@@ -308,12 +305,10 @@
     whole.wait_send()
 
 
-def return_kernel(back_ref, out_ref, send_ref, recv_ref, send_sem, recv_sem):
+def give_back(back_ref, out_ref, send_ref, recv_ref, send_sem, recv_sem):
     me = own_number()
-    barrier = announce()
     for target in range(DEVICES):
         send_ref[target] = back_ref[pl.ds(target * FEATS, FEATS), :]
-    pl.semaphore_wait(barrier, DEVICES - 1)
 
     def send(step, carry):
         send_chunk(lax.rem(me + step, DEVICES), me, send_ref, recv_ref, send_sem, recv_sem)
@@ -347,7 +342,7 @@
 GROUP_ROWS = LIST * 8
 
 
-def render_kernel(
+def composite(
     table_ref,
     list_ref,
     lane_ref,
@@ -491,10 +486,10 @@
         ones = jnp.ones((8, LANES), jnp.float32)
         image = lax.fori_loop(0, 32, forward, (ones, ones) + (zero,) * 6)[2:]
         residual = []
-        tiles = pl.ds(pl.multiple_of(group * 8, 8), 8)
         for k in range(3):
+            tiles = pl.ds(pl.multiple_of(k * TILE_DEV + group * 8, 8), 8)
             for half in range(2):
-                cols = pl.ds(k * PIX + half * LANES, LANES)
+                cols = pl.ds(half * LANES, LANES)
                 image_ref[tiles, cols] = image[k * 2 + half]
                 residual.append(image[k * 2 + half] - target_ref[tiles, cols])
 
@@ -639,11 +634,21 @@
             ]
 
 
+def shade_kernel(params_ref, index_ref, list_ref, target_ref, expand_ref, mono_ref, image_ref, out_ref, *scratch):
+    received_ref, lane_ref, row_ref, back_ref = scratch[:4]
+    deliver(params_ref, index_ref, list_ref, received_ref, lane_ref, row_ref, *scratch[4:11])
+    composite(
+        received_ref, list_ref, lane_ref, row_ref, target_ref, expand_ref, mono_ref,
+        image_ref, back_ref, *scratch[15:],
+    )
+    give_back(back_ref, out_ref, *scratch[11:15])
+
+
 SUM_PARTS = 2
 
 
 def update_kernel(
-    back_ref, index_ref, params_ref, first_ref, second_ref, rate_ref,
+    back_ref, index_ref, params_ref, first_ref, second_ref,
     new_params_ref, new_first_ref, new_second_ref,
     rows_ref, sums_ref, slope_ref, tint_ref,
 ):
@@ -716,7 +721,7 @@
                 tint = tint_ref[pl.ds((k * VIEWS + camera) * BLOCKS, BLOCKS), :]
                 slope = slope + CAMERAS[camera][4][term] * tint
             slope_ref[pl.ds(11 + 16 * k + term, BLOCKS, stride=PROWS), :] = slope
-    rates = rate_ref[...]
+    rates = rate_table()
     for block in range(BLOCKS):
         cols = pl.ds(block * LANES, LANES)
         slope = slope_ref[pl.ds(block * PROWS, PARAMS), :]
@@ -776,39 +781,27 @@
     return [chunks, chunks, pltpu.SemaphoreType.DMA, pltpu.SemaphoreType.DMA]
 
 
-def deliver(params, index, entries):
+def ordered(tile_lists):
+    return tile_lists.reshape(SLABS, 8, LIST).transpose(0, 2, 1).reshape(LANES, LANES)
+
+
+def shade(params, index, entries, target):
+    wide, narrow = expand_table()
     return run_kernel(
-        deliver_kernel,
-        [table(DEVICES * FEATS)] + [table(LANES, jnp.int32)] * 2,
+        shade_kernel,
+        [jax.ShapeDtypeStruct((3 * TILE_DEV, PIX), jnp.float32), table(DEVICES * FEATS)],
         [
+            buffer(DEVICES * FEATS, LANES),
+            buffer(LANES, LANES, dtype=jnp.int32),
+            buffer(LANES, LANES, dtype=jnp.int32),
+            buffer(DEVICES * FEATS, LANES),
             buffer(BLOCKS * PROWS, LANES),
             buffer(VIEWS * FEATS * BLOCKS, LANES),
             buffer(8 * FEATS, LANES),
         ]
-        + chunk_buffers(),
-        params,
-        index,
-        entries,
-        collective_id=0,
-    )
-
-
-def give_back(returning):
-    return run_kernel(
-        return_kernel, table(DEVICES * FEATS), chunk_buffers(), returning, collective_id=1
-    )
-
-
-def ordered(tile_lists):
-    return tile_lists.reshape(SLABS, 8, LIST).transpose(0, 2, 1).reshape(LANES, LANES)
-
-
-def render(received, entries, lanes, rows, target):
-    wide, narrow = expand_table()
-    return run_kernel(
-        render_kernel,
-        [jax.ShapeDtypeStruct((TILE_DEV, 3 * PIX), jnp.float32), table(DEVICES * FEATS)],
-        [
+        + chunk_buffers()
+        + chunk_buffers()
+        + [
             buffer(FEATS * LANES, LANES),
             buffer(LANES * KROWS, LANES),
             buffer(GROUP_ROWS, PIX),
@@ -820,13 +813,13 @@
             buffer(len(DOT_IN) * LANES, 3 * LANES, dtype=jnp.bfloat16),
             buffer(len(DOT_OUT) * LANES // 2, 2 * LANES),
         ],
-        received,
+        params,
+        index,
         entries,
-        lanes,
-        rows,
         target,
         wide,
         narrow,
+        collective_id=0,
     )
 
 
@@ -846,19 +839,17 @@
         params,
         first,
         second,
-        jnp.asarray(rate_table()),
     )
 
 
 def per_device(params, first_moment, second_moment, target_images, tile_lists, send_index):
     index = send_index[0]
     entries = ordered(tile_lists)
-    received, lanes, rows = deliver(params, index, entries)
-    target = target_images.reshape(TILE_DEV, 3 * PIX)
-    image, returning = render(received, entries, lanes, rows, target)
-    back = give_back(returning)
+    target = target_images.transpose(1, 0, 2).reshape(3 * TILE_DEV, PIX)
+    image, back = shade(params, index, entries, target)
     new_params, new_first, new_second = owner_update(back, index, params, first_moment, second_moment)
-    return (image.reshape(target_images.shape), new_params, new_first, new_second)
+    image = image.reshape(3, TILE_DEV, PIX).transpose(1, 0, 2)
+    return (image, new_params, new_first, new_second)
 
 
 def solution(mesh):

time: 126 us -> 114 us (0.905)
  Pallas kernels: 120 us -> 111 us
  local copies, waits for them, and re-layouts: 5.21 us -> 2.89 us
    pallas_call x4 -> x2, Pallas kernels: 120 us -> 111 us  [run_kernel(): pl.pallas_call(kernel, out_shape=shapes, in_specs=[WHOLE] * len(operands)...]
    reshape x2 -> x0, local copies, waits for them, and re-layouts: 3.11 us -> none  [the longest x1 1.57 us: per_device(): target = target_images.reshape(TILE_DEV, 3 * PIX)]
where the time goes in v4:
time: 114 us
  Pallas kernels  111 us (97%)
  local copies, waits for them, and re-layouts  2.89 us (3%)
    pallas_call x2, Pallas kernels, run_kernel(): pl.pallas_call(kernel, out_shape=shapes, in_specs=[WHOLE] * len(operands)...  111 us

profile of v4, /device:TPU:1, one launch (start us, length us, event | category | flops | bytes accessed | tf_op | source)
XLA Modules:
  0.0 114.2 jit_solution(6119715529787780299)
XLA Ops:
  0.6 1.2 %copy.13 = s32[4,8,512]{1,2,0:T(8,128)S(1)} copy(s32[4,8,512]{2,1,0:T(8,128)} %bitcast.14) | data formatting | bytes 131072 | tf_op jit(solution)/shard_map/reshape | solution.py:785
  1.8 1.1 reshape.21.list_ref
  2.9 98.9 %shard_map.111 = (f32[96,256]{1,0:T(8,128)}, f32[1152,128]{1,0:T(8,128)}) custom-call(f32[59,2048]{1,0:T(8,128)} %params_ref.3, s32[128,128]{1,0:T(8,128)} %bitcast.10, s32[128,128]{1,0:T(8,128)} %reshape.21.list_ref, f32[96,256]{1,0:T(8,128)} %bitcast.12, bf16[32,640]{1,0:T(8,128)(2,1)} %constant.4.clone.expand_ref, bf16[16,256]{1,0:T(8,128)(2,1)} %constant.5.clone.mono_ref), custom_call_target="tpu_custom_call" | custom-call | tf_op jit(solution)/shard_map/pallas_call | solution.py:747
  101.8 0.0 copy-start
  101.8 11.7 %shard_map.112 = (f32[59,2048]{1,0:T(8,128)}, f32[59,2048]{1,0:T(8,128)}, f32[59,2048]{1,0:T(8,128)}) custom-call(f32[1152,128]{1,0:T(8,128)} %get-tuple-element.10.back_ref, s32[128,128]{1,0:T(8,128)} %bitcast.11, f32[59,2048]{1,0:T(8,128)} %params_ref.3, f32[59,2048]{1,0:T(8,128)} %first_ref.1, f32[59,2048]{1,0:T(8,128)} %second_ref.1), custom_call_target="tpu_custom_call" | custom-call | tf_op jit(solution)/shard_map/pallas_call | solution.py:747
  113.5 0.0 copy-done
  113.6 0.6 copy.15
Async XLA Ops:
  101.8 11.8 %copy-start = (f32[96,256]{1,0:T(8,128)S(1)}, f32[96,256]{1,0:T(8,128)}, u32[]{:S(2)}) copy-start(f32[96,256]{1,0:T(8,128)} %get-tuple-element.9) | copy-start | bytes 294916

commit v5 on v4

--- a/solution.py
+++ b/solution.py
@@ -17,9 +17,10 @@
 GS_DEV = 2048
 DEVICES = 128
 CAP = 128
+TABLE_ROWS = 1168
 FEATS = 9
 BLOCKS = 16
-PROWS = 64
+PROWS = 65
 LANES = 128
 SLABS = 4
 LOG2E = 1.4426950408889634
@@ -219,6 +220,18 @@
         out_ref[pl.ds(source * FEATS, FEATS), :] = recv_ref[source]
 
 
+def order_lists(tile_ref, turned_ref, list_ref):
+    gap = jnp.zeros((LANES - 8, LANES), jnp.float32)
+    for slab in range(SLABS):
+        for block in range(LIST // LANES):
+            part = tile_ref[pl.ds(slab * 8, 8), pl.ds(block * LANES, LANES)].astype(jnp.float32)
+            turned_ref[pl.ds(block * LANES, LANES), :] = jnp.concatenate([part, gap], 0).T
+        total = turned_ref[pl.ds(0, 32, stride=16), :]
+        for place in range(1, 16):
+            total = total + pltpu.roll(turned_ref[pl.ds(place, 32, stride=16), :], 8 * place, axis=1)
+        list_ref[pl.ds(slab * 32, 32), :] = total.astype(jnp.int32)
+
+
 def invert_lists(list_ref, lane_ref, row_ref):
     sublane = lax.broadcasted_iota(jnp.int32, (LANES, LANES), 0)
     lane = lax.broadcasted_iota(jnp.int32, (LANES, LANES), 1).astype(jnp.float32)
@@ -250,7 +263,7 @@
 
 
 def deliver(
-    params_ref, index_ref, list_ref,
+    params_ref, index_ref, tile_ref, turned_ref, list_ref,
     out_ref, lane_ref, row_ref,
     rows_ref, table_ref, flat_ref, send_ref, recv_ref, send_sem, recv_sem,
 ):
@@ -297,6 +310,7 @@
             def _():
                 send_chunk(target, me, send_ref, recv_ref, send_sem, recv_sem)
 
+    order_lists(tile_ref, turned_ref, list_ref)
     invert_lists(list_ref, lane_ref, row_ref)
     whole = all_chunks(me, send_ref, recv_ref, send_sem, recv_sem)
     recv_ref[me] = send_ref[me]
@@ -338,7 +352,8 @@
 LANE_OUT = (0, 1, 5)
 DOT_OUT = (2, 3, 4, 6, 7, 8)
 KROWS = 32
-GRADS = 16
+KPITCH = 40
+GRADS = 24
 GROUP_ROWS = LIST * 8
 
 
@@ -433,10 +448,10 @@
         place = 0
         for value in values:
             for part in parts_of(value, 3):
-                coef_ref[pl.ds(octet * 8 * KROWS + place, 8, stride=KROWS), :] = part.astype(jnp.float32)
+                coef_ref[pl.ds(octet * 8 * KPITCH + place, 8, stride=KPITCH), :] = part.astype(jnp.float32)
                 place += 1
         for rest in range(place, KROWS):
-            coef_ref[pl.ds(octet * 8 * KROWS + rest, 8, stride=KROWS), :] = zero
+            coef_ref[pl.ds(octet * 8 * KPITCH + rest, 8, stride=KPITCH), :] = zero
 
     diagonal = lax.broadcasted_iota(jnp.int32, (8, LANES), 0) == lane_tile
 
@@ -446,7 +461,7 @@
         def _(quad):
             lefts = []
             for sub in range(4):
-                start = pl.multiple_of((group * 32 + quad * 4 + sub) * KROWS, KROWS)
+                start = pl.multiple_of((group * 32 + quad * 4 + sub) * KPITCH, 8)
                 lefts.append(coef_ref[pl.ds(start, KROWS), :].T.astype(jnp.bfloat16))
             wide = jnp.dot(jnp.concatenate(lefts, 0), expand_ref[...], preferred_element_type=jnp.float32)
             out = pl.ds(pl.multiple_of(quad * 512, 512), 512)
@@ -634,9 +649,11 @@
             ]
 
 
-def shade_kernel(params_ref, index_ref, list_ref, target_ref, expand_ref, mono_ref, image_ref, out_ref, *scratch):
+def shade_kernel(params_ref, index_ref, tile_ref, target_ref, expand_ref, mono_ref, image_ref, out_ref, *scratch):
+    turned_ref, list_ref = scratch[:2]
+    scratch = scratch[2:]
     received_ref, lane_ref, row_ref, back_ref = scratch[:4]
-    deliver(params_ref, index_ref, list_ref, received_ref, lane_ref, row_ref, *scratch[4:11])
+    deliver(params_ref, index_ref, tile_ref, turned_ref, list_ref, received_ref, lane_ref, row_ref, *scratch[4:11])
     composite(
         received_ref, list_ref, lane_ref, row_ref, target_ref, expand_ref, mono_ref,
         image_ref, back_ref, *scratch[15:],
@@ -657,7 +674,7 @@
     sublane = lax.broadcasted_iota(jnp.int32, (LANES, LANES), 0)
     short = lax.broadcasted_iota(jnp.int32, (BLOCKS, LANES), 0)
 
-    @pl.loop(0, VIEWS, unroll=2)
+    @pl.loop(0, VIEWS, unroll=4)
     def _(camera):
         total = jnp.zeros((SUM_PARTS * FEATS * BLOCKS, LANES), jnp.float32)
         for pair in range(4):
@@ -727,8 +744,8 @@
         slope = slope_ref[pl.ds(block * PROWS, PARAMS), :]
         new_first = beta_one * first_ref[:, cols] + (1.0 - beta_one) * slope
         new_second = beta_two * second_ref[:, cols] + (1.0 - beta_two) * slope * slope
-        first_hat = new_first / (1.0 - beta_one**adam_count)
-        second_hat = new_second / (1.0 - beta_two**adam_count)
+        first_hat = new_first * (1.0 / (1.0 - beta_one**adam_count))
+        second_hat = new_second * (1.0 / (1.0 - beta_two**adam_count))
         new_first_ref[:, cols] = new_first
         new_second_ref[:, cols] = new_second
         new_params_ref[:, cols] = params_ref[:, cols] - rates * first_hat / (
@@ -781,29 +798,27 @@
     return [chunks, chunks, pltpu.SemaphoreType.DMA, pltpu.SemaphoreType.DMA]
 
 
-def ordered(tile_lists):
-    return tile_lists.reshape(SLABS, 8, LIST).transpose(0, 2, 1).reshape(LANES, LANES)
-
-
-def shade(params, index, entries, target):
+def shade(params, index, tile_lists, target):
     wide, narrow = expand_table()
     return run_kernel(
         shade_kernel,
-        [jax.ShapeDtypeStruct((3 * TILE_DEV, PIX), jnp.float32), table(DEVICES * FEATS)],
+        [jax.ShapeDtypeStruct((3 * TILE_DEV, PIX), jnp.float32), table(TABLE_ROWS)],
         [
-            buffer(DEVICES * FEATS, LANES),
+            buffer(LIST, LANES),
+            buffer(LANES, LANES, dtype=jnp.int32),
+            buffer(TABLE_ROWS, LANES),
             buffer(LANES, LANES, dtype=jnp.int32),
             buffer(LANES, LANES, dtype=jnp.int32),
-            buffer(DEVICES * FEATS, LANES),
+            buffer(TABLE_ROWS, LANES),
             buffer(BLOCKS * PROWS, LANES),
             buffer(VIEWS * FEATS * BLOCKS, LANES),
-            buffer(8 * FEATS, LANES),
+            buffer(80, LANES),
         ]
         + chunk_buffers()
         + chunk_buffers()
         + [
             buffer(FEATS * LANES, LANES),
-            buffer(LANES * KROWS, LANES),
+            buffer(LANES * KPITCH, LANES),
             buffer(GROUP_ROWS, PIX),
             buffer(GROUP_ROWS, PIX),
             buffer(GROUP_ROWS, 3 * LANES),
@@ -815,7 +830,7 @@
         ],
         params,
         index,
-        entries,
+        tile_lists,
         target,
         wide,
         narrow,
@@ -844,9 +859,8 @@
 
 def per_device(params, first_moment, second_moment, target_images, tile_lists, send_index):
     index = send_index[0]
-    entries = ordered(tile_lists)
     target = target_images.transpose(1, 0, 2).reshape(3 * TILE_DEV, PIX)
-    image, back = shade(params, index, entries, target)
+    image, back = shade(params, index, tile_lists, target)
     new_params, new_first, new_second = owner_update(back, index, params, first_moment, second_moment)
     image = image.reshape(3, TILE_DEV, PIX).transpose(1, 0, 2)
     return (image, new_params, new_first, new_second)

time: 114 us -> 107 us (0.939)
  Pallas kernels: 111 us -> 105 us
  local copies, waits for them, and re-layouts: 2.89 us -> 0.65 us
    pallas_call x2, Pallas kernels: 111 us -> 105 us  [run_kernel(): pl.pallas_call(kernel, out_shape=shapes, in_specs=[WHOLE] * len(operands)...]
    reshape x2 -> x0, local copies, waits for them, and re-layouts: 2.25 us -> none  [ordered(): tile_lists.reshape(SLABS, 8, LIST).transpose(0, 2, 1).reshape(LANES, LANES)]
where the time goes in v5:
time: 107 us; the launch traced here: 106 us
  Pallas kernels  105 us (98%)
    pallas_call x2, Pallas kernels, run_kernel(): pl.pallas_call(kernel, out_shape=shapes, in_specs=[WHOLE] * len(operands)...  105 us

profile of v5, /device:TPU:1, one launch (start us, length us, event | category | flops | bytes accessed | tf_op | source)
XLA Modules:
  0.0 106.4 jit_solution(16747443293827097258)
XLA Ops:
  0.6 97.6 %shard_map.111 = (f32[96,256]{1,0:T(8,128)}, f32[1168,128]{1,0:T(8,128)}) custom-call(f32[59,2048]{1,0:T(8,128)} %params_ref.3, s32[128,128]{1,0:T(8,128)} %bitcast.7, s32[32,512]{1,0:T(8,128)} %tile_ref.1, f32[96,256]{1,0:T(8,128)} %bitcast.9, bf16[32,640]{1,0:T(8,128)(2,1)} %constant.4.clone.expand_ref, bf16[16,256]{1,0:T(8,128)(2,1)} %constant.5.clone.mono_ref), custom_call_target="tpu_custom_call" | custom-call | tf_op jit(solution)/shard_map/pallas_call | solution.py:764
  98.3 0.0 copy-start
  98.3 7.5 %shard_map.112 = (f32[59,2048]{1,0:T(8,128)}, f32[59,2048]{1,0:T(8,128)}, f32[59,2048]{1,0:T(8,128)}) custom-call(f32[1168,128]{1,0:T(8,128)} %get-tuple-element.10.back_ref, s32[128,128]{1,0:T(8,128)} %bitcast.8, f32[59,2048]{1,0:T(8,128)} %params_ref.3, f32[59,2048]{1,0:T(8,128)} %first_ref.1, f32[59,2048]{1,0:T(8,128)} %second_ref.1), custom_call_target="tpu_custom_call" | custom-call | tf_op jit(solution)/shard_map/pallas_call | solution.py:764
  105.8 0.0 copy-done
  105.8 0.6 copy.13
Async XLA Ops:
  98.3 7.5 %copy-start = (f32[96,256]{1,0:T(8,128)S(1)}, f32[96,256]{1,0:T(8,128)}, u32[]{:S(2)}) copy-start(f32[96,256]{1,0:T(8,128)} %get-tuple-element.9) | copy-start | bytes 294916

commit v6 on v5

--- a/solution.py
+++ b/solution.py
@@ -457,7 +457,7 @@
 
     @pl.loop(0, SLABS)
     def _(group):
-        @pl.loop(0, 8, unroll=4)
+        @pl.loop(0, 8, unroll=8)
         def _(quad):
             lefts = []
             for sub in range(4):
@@ -499,7 +499,7 @@
             return tuple(through + image)
 
         ones = jnp.ones((8, LANES), jnp.float32)
-        image = lax.fori_loop(0, 32, forward, (ones, ones) + (zero,) * 6)[2:]
+        image = lax.fori_loop(0, 32, forward, (ones, ones) + (zero,) * 6, unroll=2)[2:]
         residual = []
         for k in range(3):
             tiles = pl.ds(pl.multiple_of(k * TILE_DEV + group * 8, 8), 8)
@@ -546,9 +546,9 @@
         stack = jnp.concatenate([stack, stack], 1)
         powers = jnp.concatenate([mono_ref[...], mono_ref[...]], 1)
 
-        @pl.loop(0, 2)
+        @pl.loop(0, 1)
         def _(chunk):
-            rows = pl.ds(pl.multiple_of(chunk * 2048, 2048), 2048)
+            rows = pl.ds(pl.multiple_of(chunk * 4096, 4096), 4096)
             moments = lax.dot_general(
                 powers, push_ref[rows, pl.ds(0, 2 * PIX)], CONTRACT, preferred_element_type=jnp.float32
             )
@@ -556,9 +556,9 @@
                 stack, push_ref[rows, pl.ds(2 * PIX, 2 * PIX)], CONTRACT, preferred_element_type=jnp.float32
             )
             tints = tints[:24] + tints[24:]
-            for line in range(16):
+            for line in range(32):
                 cols = slice(line * LANES, (line + 1) * LANES)
-                base = ((group * 32) + chunk * 16 + line) * GRADS
+                base = ((group * 32) + chunk * 32 + line) * GRADS
                 moment_ref[pl.ds(pl.multiple_of(base, 8), 8), :] = moments[:8, cols]
                 for k in range(3):
                     own = jnp.where(diagonal, tints[k * 8 : k * 8 + 8, cols], 0.0)

time: 107 us -> 105 us (0.981)
  Pallas kernels: 105 us -> 103 us
    pallas_call x2, Pallas kernels: 105 us -> 103 us  [run_kernel(): pl.pallas_call(kernel, out_shape=shapes, in_specs=[WHOLE] * len(operands)...]
where the time goes in v6:
time: 105 us
  Pallas kernels  103 us (98%)
    pallas_call x2, Pallas kernels, run_kernel(): pl.pallas_call(kernel, out_shape=shapes, in_specs=[WHOLE] * len(operands)...  103 us

profile of v6, /device:TPU:1, one launch (start us, length us, event | category | flops | bytes accessed | tf_op | source)
XLA Modules:
  0.0 104.6 jit_solution(5886616115421731813)
XLA Ops:
  0.6 95.8 %shard_map.111 = (f32[96,256]{1,0:T(8,128)}, f32[1168,128]{1,0:T(8,128)}) custom-call(f32[59,2048]{1,0:T(8,128)} %params_ref.3, s32[128,128]{1,0:T(8,128)} %bitcast.7, s32[32,512]{1,0:T(8,128)} %tile_ref.1, f32[96,256]{1,0:T(8,128)} %bitcast.9, bf16[32,640]{1,0:T(8,128)(2,1)} %constant.4.clone.expand_ref, bf16[16,256]{1,0:T(8,128)(2,1)} %constant.5.clone.mono_ref), custom_call_target="tpu_custom_call" | custom-call | tf_op jit(solution)/shard_map/pallas_call | solution.py:764
  96.5 0.0 copy-start
  96.5 7.5 %shard_map.112 = (f32[59,2048]{1,0:T(8,128)}, f32[59,2048]{1,0:T(8,128)}, f32[59,2048]{1,0:T(8,128)}) custom-call(f32[1168,128]{1,0:T(8,128)} %get-tuple-element.10.back_ref, s32[128,128]{1,0:T(8,128)} %bitcast.8, f32[59,2048]{1,0:T(8,128)} %params_ref.3, f32[59,2048]{1,0:T(8,128)} %first_ref.1, f32[59,2048]{1,0:T(8,128)} %second_ref.1), custom_call_target="tpu_custom_call" | custom-call | tf_op jit(solution)/shard_map/pallas_call | solution.py:764
  104.0 0.0 copy-done
  104.0 0.6 copy.13
Async XLA Ops:
  96.5 7.5 %copy-start = (f32[96,256]{1,0:T(8,128)S(1)}, f32[96,256]{1,0:T(8,128)}, u32[]{:S(2)}) copy-start(f32[96,256]{1,0:T(8,128)} %get-tuple-element.9) | copy-start | bytes 294916
